TPU v7x, 128 devices: a whole 4x4x4 slice. The times are simulated.
128 devices in a mesh: row: 8 (over x, y_lo), col: 16 (over z, y_hi, core).
Axes of the slice: x: 4, y: 4 (y_hi: 2, y_lo: 2; y = y_hi * 2 + y_lo), z: 4, core: 2. Of those that a mesh axis runs over, the one named last changes fastest.
Arguments:
- dense_in: bfloat16 [1024, 28672], P('col', 'row'), may hold values from -6 to 6
- pruned_in: bfloat16 [1024, 28672], P('col', 'row'), may hold values from -6 to 6
- weight: bfloat16 [28672, 8192], P('row', 'col'), may hold values from -0.03125 to 0.03125
- keep_bits: int32 [512, 28672], P('col', 'row'), may hold values from 0 to 65535
Outputs:
- gram_tile: float32 [8192, 8192], P('row', 'col')
- cross_tile: float32 [8192, 8192], P('row', 'col')
Inputs may be any that keep to these rules, and one draw needn't show every extreme that they name: `keep_bits`: each word holds 16 independent flags, each 1 with probability one half.
All inputs are finite; a program needn't handle non-finite values.
Results may differ from a plain program's by a relative error of at most 0.0039.
Values may be sent and summed in bfloat16 or wider, within the bound.
No kernel may reach another device: no remote copies, remote signals or barrier semaphores. Data moves between devices by JAX's collectives and lax.ppermute only.
A program may use at most 128 MiB of HBM per device.

v0:
```python
import jax
import jax.numpy as jnp
from jax import lax
from jax.sharding import Mesh
from jax.sharding import PartitionSpec as P

ROW = ("row_0", "row_1")


def sent_together(arrays, axis, dim, along):
    both = jnp.concatenate(arrays, axis=along)
    result, at, finished = (lax.all_gather(both, axis, axis=dim, tiled=True), 0, [])
    for a in arrays:
        finished.append(lax.slice_in_dim(result, at, at + a.shape[along], axis=along))
        at += a.shape[along]
    return tuple(finished)


def split_up(shard, dim, peers):
    before, after = (shard.shape[:dim], shard.shape[dim + 1 :])
    return jnp.moveaxis(shard.reshape(*before, peers, -1, *after), dim, 0)


def summed_on_arrival(shard, axis, dim):
    peers = lax.axis_size(axis)
    pieces = lax.all_to_all(split_up(shard, dim, peers), axis, 0, 0, tiled=True)
    return jnp.sum(pieces, axis=0)


def gather_axes(shard, axes, dim):
    result = shard
    for number in range(len(axes) - 1, -1, -1):
        result = lax.all_gather(result, axes[number], axis=dim, tiled=True)
    return result


def from_root(shard, axis, root):
    mine = lax.axis_index(axis) == root
    return lax.psum(jnp.where(mine, shard, jnp.zeros_like(shard)), axis)


def unpack_block(word_block):
    shifts = jnp.arange(16, dtype=jnp.int32)
    flag_bits = jnp.right_shift(word_block[:, None, :], shifts[None, :, None]) & 1
    return flag_bits.reshape(word_block.shape[0] * 16, word_block.shape[1])


def local(dense_in, pruned_in, weight, keep_bits):
    keep_flags = unpack_block(keep_bits)
    pruned_w = jnp.where(keep_flags.T == 1, weight, jnp.zeros_like(weight))
    dense_all, pruned_all = sent_together((dense_in, pruned_in), "col", 0, 1)
    pruned_part = jnp.dot(pruned_all, pruned_w, preferred_element_type=jnp.float32)
    dense_part = jnp.dot(dense_all, weight, preferred_element_type=jnp.float32)
    partials = jnp.stack([dense_part - pruned_part, pruned_part])
    shares = summed_on_arrival(partials, ROW, 1)
    stacked = gather_axes(shares.astype(jnp.bfloat16), ROW, 1)
    per_row = lax.axis_size("col") // lax.axis_size(ROW)
    panel_list = []
    for offset in range(per_row):
        source = per_row * lax.axis_index(ROW) + offset
        panel_list.append(from_root(stacked, "col", source))
    panels = jnp.concatenate(panel_list, 2)
    pruned_cols = stacked[1]
    tokens = dense_in.shape[0] * lax.axis_size("col")
    dims = (((0,), (0,)), ((), ()))
    gram_tile = (
        lax.dot_general(panels[1], pruned_cols, dims, preferred_element_type=jnp.float32) / tokens
    )
    cross_tile = (
        lax.dot_general(panels[0], pruned_cols, dims, preferred_element_type=jnp.float32) / tokens
    )
    return (gram_tile, cross_tile)


def solution(mesh):
    split = Mesh(mesh.devices.reshape(4, 2, mesh.shape["col"]), ("row_0", "row_1", "col"))
    in_specs = (P("col", ROW), P("col", ROW), P(ROW, "col"), P("col", ROW))
    out_specs = (P(ROW, "col"), P(ROW, "col"))
    return jax.shard_map(local, mesh=split, in_specs=in_specs, out_specs=out_specs, check_vma=False)
```

profile of v0, /device:TPU:1, one launch (start us, length us, event | category | flops | bytes accessed | tf_op | source)
XLA Modules:
  0.0 395.5 jit_solution(4037303946099783191)
XLA Ops:
  7.2 0.0 all-gather.3.cloned.1.call-start
  7.2 2.1 pad_maximum_fusion
  9.4 0.0 all-gather.3.cloned.1.call-update
  9.4 0.0 copy-start.3
  9.4 0.0 all-gather.5.cloned.1.call-start
  9.4 6.0 %copy.8 = bf16[3584,512]{0,1:T(8,128)(2,1)} copy(bf16[3584,512]{1,0:T(8,128)(2,1)} %param.6) | data formatting | bytes 7340032 | tf_op args[2]
  15.4 0.1 shift_right_arithmetic.23
  15.5 0.0 copy-done.3
  15.5 1.7 fusion.5
  17.2 97.4 %all-gather.3.cloned.1.call-done = bf16[1024,7168]{1,0:T(8,128)(2,1)} async-done(((bf16[64,7168]{1,0:T(8,128)(2,1)}), bf16[1024,7168]{1,0:T(8,128)(2,1)}) %all-gather.3.cloned.1.call-update) | async-done | bytes 14680080 | tf_op jit(solution)/shard_map/all_gather | solution.py:12
  114.6 0.0 copy-start
  114.6 0.0 copy-start.4
  114.6 7.5 %fusion = f32[1024,512]{1,0:T(8,128)S(1)} fusion(bf16[1024,7168]{1,0:T(8,128)(2,1)} %all-gather.3.cloned.1.call-done, bf16[3584,512]{0,1:T(8,128)(2,1)} %copy.8, pred[512,3584]{1,0:T(32,128)(4,1)S(1)} %fusion.5), kind=kOutput, calls=%fused_computation | convolution fusion | flops 3759931392 | bytes 14942208 | tf_op jit(solution)/shard_map/dot_general | solution.py:52
  122.1 0.0 copy-done
  122.1 1.9 copy-done.4
  124.0 3.9 fusion.11
  128.0 0.6 maximum_bitcast_fusion
  128.6 52.0 %all_to_all.5 = f32[8,2,128,512]{3,2,1,0:T(8,128)} all-to-all(f32[8,2,128,512]{3,2,1,0:T(8,128)S(1)} %maximum_bitcast_fusion), channel_id=1, replica_groups=mesh['row_0'=4,'row_1'=2,'col'=16] {'row_0','row_1'}, dimensions={0} | all-to-all | bytes 8388608 | tf_op jit(solution)/shard_map/all_to_all | solution.py:26
  180.6 2.7 reduce_sum.9
  183.3 6.6 %all_gather.10 = bf16[2,256,512]{2,1,0:T(8,128)(2,1)} all-gather(bf16[2,128,512]{2,1,0:T(8,128)(2,1)S(1)} %reduce_sum.9), channel_id=1, replica_groups=mesh['row_0'=4,'row_1'=2,'col'=16] {'row_1'}, dimensions={1}, use_global_device_ids=true | all-gather | bytes 786432 | tf_op jit(solution)/shard_map/all_gather | solution.py:33
  189.9 0.0 all-gather.5.cloned.1.call-update
  189.9 0.0 all-reduce.3.cloned.1.call-start
  190.0 30.2 %all-gather.5.cloned.1.call-done = bf16[2,1024,512]{2,1,0:T(8,128)(2,1)} async-done(((bf16[2,256,512]{2,1,0:T(8,128)(2,1)}), bf16[2,1024,512]{2,1,0:T(8,128)(2,1)}) %all-gather.5.cloned.1.call-update) | async-done | bytes 2097168 | tf_op jit(solution)/shard_map/all_gather | solution.py:33
  220.2 3.9 broadcast_select_fusion
  224.0 0.0 all-reduce.3.cloned.1.call-update
  224.1 155.9 %all-reduce.3.cloned.1.call-done = (bf16[2,1024,512]{2,1,0:T(8,128)(2,1)}, bf16[2,1024,512]{2,1,0:T(8,128)(2,1)}) async-done(((bf16[2,1024,512]{2,1,0:T(8,128)(2,1)}, bf16[2,1024,512]{2,1,0:T(8,128)(2,1)}), (bf16[2,1024,512]{2,1,0:T(8,128)(2,1)}, bf16[2,1024,512]{2,1,0:T(8,128)(2,1)})) %all-reduce.3.cloned.1.call-update) | async-done | bytes 4194320 | tf_op jit(solution)/shard_map/psum | solution.py:39
  379.9 0.0 copy-start.2
  379.9 2.1 constant_dynamic-update-slice_fusion.1
  382.0 0.2 copy-done.2
  382.2 0.0 copy-start.1
  382.2 0.3 constant_dynamic-update-slice_fusion
  382.5 1.3 copy-done.1
  383.7 2.6 fusion.9
  386.3 2.6 fusion.10
  (1 shorter events, 0.0 us)
Async XLA Ops:
  7.2 107.4 %all-gather.3.cloned.1.call-start = ((), (), s32[]{:S(2)}) async-start(), calls=%async_computation.1 | async-start | bytes 15597568 | tf_op jit(solution)/shard_map/all_gather | solution.py:12
  9.4 6.1 %copy-start.3 = (s32[32,3584]{1,0:T(8,128)S(1)}, s32[32,3584]{1,0:T(8,128)}, u32[]{:S(2)}) copy-start(s32[32,3584]{1,0:T(8,128)} %param.7) | copy-start | bytes 1376260
  9.4 210.8 %all-gather.5.cloned.1.call-start = ((), (), s32[]{:S(2)}) async-start(), calls=%async_computation.2 | async-start | bytes 2621440 | tf_op jit(solution)/shard_map/all_gather | solution.py:33
  114.6 7.6 %copy-start = (bf16[3584,512]{1,0:T(8,128)(2,1)S(1)}, bf16[3584,512]{1,0:T(8,128)(2,1)}, u32[]{:S(2)}) copy-start(bf16[3584,512]{1,0:T(8,128)(2,1)} %param.6) | copy-start | bytes 11010052
  114.6 9.5 %copy-start.4 = (bf16[1024,7168]{1,0:T(8,128)(2,1)S(1)}, bf16[1024,7168]{1,0:T(8,128)(2,1)}, u32[]{:S(2)}) copy-start(bf16[1024,7168]{1,0:T(8,128)(2,1)} %all-gather.3.cloned.1.call-done) | copy-start | bytes 44040196
  189.9 190.0 %all-reduce.3.cloned.1.call-start = ((), (), s32[]{:S(2)}) async-start(), calls=%async_computation.3 | async-start | bytes 8388608 | tf_op jit(solution)/shard_map/psum | solution.py:39
  379.9 2.2 copy-start.2
  382.2 1.6 copy-start.1
Sparse Core Ops, SparseCore 0:
  11.0 103.4 all-gather.2
  190.0 30.0 all-gather.4
  224.2 155.6 all-reduce.2
where the time goes:
time: 397 us; the launch traced here: 395 us
  waiting for transfers between devices  283 us (71%)
  blocking collectives  58.6 us (15%)
  matrix products  16.7 us (4%)
  between operations  13.8 us (3%)
  local copies, waits for them, and re-layouts  11.8 us (3%)
  other arithmetic  11 us (3%)
    psum x1, waiting for transfers between devices, from_root(): return lax.psum(jnp.where(mine, shard, jnp.zeros_like(shard)), axis)  156 us
    all_gather x1, waiting for transfers between devices, sent_together(): lax.all_gather(both, axis, axis=dim, tiled=True)  97.4 us
    all_to_all x1, blocking collectives, summed_on_arrival(): pieces = lax.all_to_all(split_up(shard, dim, peers), axis, 0, 0, tiled=True)  52 us
    all_gather x1, waiting for transfers between devices, gather_axes(): result = lax.all_gather(result, axes[number], axis=dim, tiled=True)  30.2 us
    unnamed x12, local copies, waits for them, and re-layouts  11.4 us
  transfers between devices with their start and end apart: 3, of which 3 were waited for; matrix products, arithmetic and copies ran while one was open for 2% of the time, Pallas kernels for 0%

commit v1 on v0

v1 whole, which is shorter than its diff:
```python
import jax
import jax.numpy as jnp
from jax import lax
from jax.sharding import Mesh
from jax.sharding import PartitionSpec as P

ROW = ("x", "yl")
SIDE = ("z", "yh")
COL = ("z", "yh", "k")
BF = jnp.bfloat16
F32 = jnp.float32


def step(a, dz, dy):
    nz, ny = lax.axis_size("z"), lax.axis_size("yh")
    pairs = [
        (z * ny + y, ((z + dz) % nz) * ny + (y + dy) % ny) for z in range(nz) for y in range(ny)
    ]
    return lax.ppermute(a, SIDE, pairs)


def swap(a):
    return lax.ppermute(a, "k", [(0, 1), (1, 0)])


def gathered(own):
    half = own.shape[0] // 2
    up, down = step(own, 1, 0), step(own, 3, 0)
    side = step(own, 0, 1)
    far = jnp.concatenate([step(up[:half], 1, 0), step(down[half:], 3, 0)], 0)
    side_up, side_down = step(side, 1, 0), step(side, 3, 0)
    side_far = step(far, 0, 1)
    return [own, side, down, side_down, far, side_far, up, side_up]


def transposed(a):
    pairs = []
    for r in range(8):
        for c in range(8):
            for k in range(2):
                pairs.append(((r * 8 + c) * 2 + k, (c * 8 + r) * 2 + k))
    return lax.ppermute(a, ROW + COL, pairs)


def spread(a, axes):
    n = lax.axis_size(axes)
    return lax.all_to_all(jnp.broadcast_to(a, (n,) + a.shape), axes, 0, 0, tiled=True)


def keep_mask(words):
    shifts = jnp.arange(16, dtype=jnp.int32)
    bits = jnp.right_shift(words[:, None, :], shifts[None, :, None]) & 1
    return bits.reshape(words.shape[0] * 16, words.shape[1]).T == 1


def dots(blocks, mine, other):
    out = []
    for part in (blocks[:4], blocks[4:]):
        a = jnp.concatenate(part, 0)
        halves = [jnp.dot(a, w, preferred_element_type=F32) for w in (mine, other)]
        out.append(jnp.concatenate(halves, 1))
    return jnp.concatenate(out, 0).reshape(8, -1, 2 * mine.shape[1])


def summed(partial):
    z, yh = lax.axis_index("z"), lax.axis_index("yh")
    me = lax.axis_index(ROW)
    order = [((place // 2 - z) % 4) * 2 + (place % 2 - yh) % 2 for place in range(8)]
    sent = jnp.stack([lax.dynamic_index_in_dim(partial, i, 0, False).astype(BF) for i in order])
    at_me = ((me // 2 - z) % 4) * 2 + (me % 2 - yh) % 2
    own = lax.dynamic_index_in_dim(partial, at_me, 0, False)
    came = lax.all_to_all(sent, ROW, 0, 0, tiled=True)
    rest = own - own.astype(BF).astype(F32)
    total = jnp.sum(came.astype(F32), 0) + rest
    half = total.shape[1] // 2
    swapped = jnp.concatenate([total[:, half:], total[:, :half]], 1)
    return jnp.where(lax.axis_index("k") == 0, total, swapped).astype(BF)


def both(own):
    return jnp.concatenate([own, swap(own)], 0)


def columns(p):
    every = spread(p, ROW).reshape(-1, p.shape[1])
    k = lax.axis_index("k")
    half = p.shape[1] // 2
    mine = lax.dynamic_slice_in_dim(every, k * half, half, 1)
    others = lax.dynamic_slice_in_dim(every, (1 - k) * half, half, 1)
    return jnp.concatenate([mine, swap(others)], 0)


def rows(s):
    every = spread(transposed(s), SIDE)
    return both(every.reshape(-1, s.shape[1]))


def local(dense_in, pruned_in, weight, keep_bits):
    tokens = dense_in.shape[0] * lax.axis_size(COL)
    pruned_blocks = gathered(pruned_in)
    pruned_w = jnp.where(keep_mask(keep_bits), weight, jnp.zeros_like(weight))
    pruned_part = dots(pruned_blocks, pruned_w, swap(pruned_w))
    dense_blocks = gathered(dense_in)
    dense_part = dots(dense_blocks, weight, swap(weight))
    p = summed(pruned_part)
    cols = columns(p)
    rows_p = rows(p)
    d = summed(dense_part - pruned_part)
    rows_d = rows(d)
    dims = (((0,), (0,)), ((), ()))
    gram_tile = lax.dot_general(rows_p, cols, dims, preferred_element_type=F32) / tokens
    cross_tile = lax.dot_general(rows_d, cols, dims, preferred_element_type=F32) / tokens
    return (gram_tile, cross_tile)


def solution(mesh):
    split = Mesh(mesh.devices.reshape(4, 2, 4, 2, 2), ROW + COL)
    in_specs = (P(COL, ROW), P(COL, ROW), P(ROW, COL), P(COL, ROW))
    out_specs = (P(ROW, COL), P(ROW, COL))
    return jax.shard_map(local, mesh=split, in_specs=in_specs, out_specs=out_specs, check_vma=False)
```

time: 397 us -> 212 us (0.53)
  waiting for transfers between devices: 283 us -> 78.2 us
  starting transfers between devices: 0.12 us -> 54.8 us
  blocking collectives: 58.6 us -> 32.7 us
  between operations: 13.8 us -> 1.11 us
  local copies, waits for them, and re-layouts: 11.8 us -> 21.6 us
  other arithmetic: 11 us -> 6.7 us
    psum x1 -> x0, waiting for transfers between devices: 156 us -> none  [from_root(): return lax.psum(jnp.where(mine, shard, jnp.zeros_like(shard)), axis)]
    all_gather x2 -> x0, waiting for transfers between devices: 128 us -> none  [the longest x1 97.4 us: sent_together(): lax.all_gather(both, axis, axis=dim, tiled=True)]
    ppermute x0 -> x23, waiting for transfers between devices: none -> 42.8 us  [the longest x16 41.3 us: step(): return lax.ppermute(a, SIDE, pairs)]
    all_to_all x0 -> x4, waiting for transfers between devices: none -> 35.4 us  [the longest x2 21.2 us: spread(): lax.all_to_all(jnp.broadcast_to(a, (n,) + a.shape), axes, 0, 0, tiled=True)]
    ppermute x0 -> x23, starting transfers between devices: none -> 32.2 us  [the longest x16 22.4 us: step(): return lax.ppermute(a, SIDE, pairs)]
    all_to_all x0 -> x4, starting transfers between devices: none -> 22.5 us  [the longest x2 14.3 us: spread(): lax.all_to_all(jnp.broadcast_to(a, (n,) + a.shape), axes, 0, 0, tiled=True)]
    all_to_all x1, blocking collectives: 52 us -> 32.7 us  [spread(): lax.all_to_all(jnp.broadcast_to(a, (n,) + a.shape), axes, 0, 0, tiled=True)]
    all_gather x1 -> x0, blocking collectives: 6.65 us -> none  [gather_axes(): result = lax.all_gather(result, axes[number], axis=dim, tiled=True)]
  transfers between devices with their start and end apart: 3 -> 27, of which waited for: 3 -> 14; matrix products, arithmetic and copies ran while one was open for 2% -> 14% of each run, Pallas kernels for 0% -> 0%
where the time goes in v1:
time: 212 us
  waiting for transfers between devices  78.2 us (37%)
  starting transfers between devices  54.8 us (26%)
  blocking collectives  32.7 us (15%)
  local copies, waits for them, and re-layouts  21.6 us (10%)
  matrix products  16.6 us (8%)
  other arithmetic  6.7 us (3%)
    ppermute x16, waiting for transfers between devices, step(): return lax.ppermute(a, SIDE, pairs)  41.3 us
    all_to_all x1, blocking collectives, spread(): lax.all_to_all(jnp.broadcast_to(a, (n,) + a.shape), axes, 0, 0, tiled=True)  32.7 us
    ppermute x16, starting transfers between devices, step(): return lax.ppermute(a, SIDE, pairs)  22.4 us
    all_to_all x2, waiting for transfers between devices, spread(): lax.all_to_all(jnp.broadcast_to(a, (n,) + a.shape), axes, 0, 0, tiled=True)  21.2 us
    unnamed x39, local copies, waits for them, and re-layouts  17.6 us
    all_to_all x2, starting transfers between devices, spread(): lax.all_to_all(jnp.broadcast_to(a, (n,) + a.shape), axes, 0, 0, tiled=True)  14.3 us
    all_to_all x2, waiting for transfers between devices, summed(): came = lax.all_to_all(sent, ROW, 0, 0, tiled=True)  14.3 us
    dot_general x8, matrix products, dots(): halves = [jnp.dot(a, w, preferred_element_type=F32) for w in (mine, other)]  8.95 us
  transfers between devices with their start and end apart: 27, of which 14 were waited for; matrix products, arithmetic and copies ran while one was open for 14% of the time, Pallas kernels for 0%

profile of v1, /device:TPU:1, one launch (start us, length us, event | category | flops | bytes accessed | tf_op | source)
XLA Modules:
  0.0 211.7 jit_solution(2435112205139751630)
XLA Ops:
  0.6 2.5 %collective-permute-start.4 = (bf16[64,3584]{1,0:T(8,128)(2,1)}, bf16[64,3584]{1,0:T(8,128)(2,1)S(1)}, u32[]{:S(2)}, u32[]{:S(2)}) collective-permute-start(bf16[64,3584]{1,0:T(8,128)(2,1)} %param.5), channel_id=1, source_target_pairs={{0,4},{2,6},{4,8},{6,10},{8,12},{10,14},{12,0},{14,2},{1,5},{3,7},... | collective-permute-start | bytes 1376264 | tf_op jit(solution)/shard_map/ppermute | solution.py:19
  3.2 2.2 %collective-permute-start.1 = (bf16[64,3584]{1,0:T(8,128)(2,1)}, bf16[64,3584]{1,0:T(8,128)(2,1)S(1)}, u32[]{:S(2)}, u32[]{:S(2)}) collective-permute-start(bf16[64,3584]{1,0:T(8,128)(2,1)} %param.5), channel_id=1, source_target_pairs={{0,12},{2,14},{4,0},{6,2},{8,4},{10,6},{12,8},{14,10},{1,13},{3,15... | collective-permute-start | bytes 1376264 | tf_op jit(solution)/shard_map/ppermute | solution.py:19
  5.4 2.9 %collective-permute-start = (bf16[64,3584]{1,0:T(8,128)(2,1)}, bf16[64,3584]{1,0:T(8,128)(2,1)S(1)}, u32[]{:S(2)}, u32[]{:S(2)}) collective-permute-start(bf16[64,3584]{1,0:T(8,128)(2,1)} %param.5), channel_id=1, source_target_pairs={{0,2},{2,0},{4,6},{6,4},{8,10},{10,8},{12,14},{14,12},{1,3},{3,1},... | collective-permute-start | bytes 1376264 | tf_op jit(solution)/shard_map/ppermute | solution.py:19
  8.3 2.7 %collective-permute-start.13 = (bf16[64,3584]{1,0:T(8,128)(2,1)}, bf16[64,3584]{1,0:T(8,128)(2,1)S(1)}, u32[]{:S(2)}, u32[]{:S(2)}) collective-permute-start(bf16[64,3584]{1,0:T(8,128)(2,1)} %param.4), channel_id=1, source_target_pairs={{0,12},{2,14},{4,0},{6,2},{8,4},{10,6},{12,8},{14,10},{1,13},{3,15... | collective-permute-start | bytes 1376264 | tf_op jit(solution)/shard_map/ppermute | solution.py:19
  11.0 1.8 constant_dynamic-update-slice_fusion.3
  12.8 5.9 %copy.7 = bf16[3584,512]{0,1:T(8,128)(2,1)} copy(bf16[3584,512]{1,0:T(8,128)(2,1)} %param.6) | data formatting | bytes 7340032 | tf_op args[2]
  18.8 3.2 %bitcast_select_fusion = bf16[3584,512]{0,1:T(8,128)(2,1)S(1)} fusion(bf16[3584,512]{0,1:T(8,128)(2,1)} %copy.7, s32[512]{0:T(512)S(1)} %shift_right_arithmetic.23, s32[32,3584]{1,0:T(8,128)S(1)} %copy-done.3), kind=kLoop, calls=%fused_computation.3 | loop fusion | flops 7340032 | bytes 7800832 | tf_op jit(solution)/shard_map/jit(_where)/select_n | solution.py:101
  22.3 2.2 %collective-permute-start.15 = (bf16[3584,512]{1,0:T(8,128)(2,1)S(1)}, bf16[3584,512]{1,0:T(8,128)(2,1)S(1)}, u32[]{:S(2)}, u32[]{:S(2)}) collective-permute-start(bf16[3584,512]{1,0:T(8,128)(2,1)S(1)} %copy-done.1), channel_id=1, source_target_pairs={{0,1},{1,0},{2,3},{3,2},{4,5},{5,4},{6,7},{7,6},{8,9},{9,8},{10,11... | collective-permute-start | bytes 11010056 | tf_op jit(solution)/shard_map/ppermute | solution.py:23
  24.5 1.1 collective-permute-done.16
  25.6 1.2 collective-permute-start.3
  27.0 6.9 %collective-permute-done.12 = bf16[64,3584]{1,0:T(8,128)(2,1)S(1)} collective-permute-done((bf16[64,3584]{1,0:T(8,128)(2,1)S(1)}, bf16[64,3584]{1,0:T(8,128)(2,1)S(1)}, u32[]{:S(2)}, u32[]{:S(2)}) %collective-permute-start.12) | collective-permute-done | bytes 458784 | tf_op jit(solution)/shard_map/ppermute | solution.py:19
  33.9 1.5 collective-permute-start.17
  35.5 1.3 collective-permute-start.18
  36.9 1.9 collective-permute-done.6
  38.8 1.3 collective-permute-done.17
  40.1 1.5 collective-permute-start.2
  41.6 1.6 collective-permute-done.18
  43.3 9.8 %collective-permute-done.2 = bf16[64,3584]{1,0:T(8,128)(2,1)S(1)} collective-permute-done((bf16[64,3584]{1,0:T(8,128)(2,1)S(1)}, bf16[64,3584]{1,0:T(8,128)(2,1)S(1)}, u32[]{:S(2)}, u32[]{:S(2)}) %collective-permute-start.2) | collective-permute-done | bytes 458784 | tf_op jit(solution)/shard_map/ppermute | solution.py:19
  53.4 8.6 %collective-permute-done.14 = bf16[64,3584]{1,0:T(8,128)(2,1)S(1)} collective-permute-done((bf16[64,3584]{1,0:T(8,128)(2,1)S(1)}, bf16[64,3584]{1,0:T(8,128)(2,1)S(1)}, u32[]{:S(2)}, u32[]{:S(2)}) %collective-permute-start.14) | collective-permute-done | bytes 458784 | tf_op jit(solution)/shard_map/ppermute | solution.py:19
  62.0 3.5 %collective-permute-start.7 = (bf16[64,3584]{1,0:T(8,128)(2,1)S(1)}, bf16[64,3584]{1,0:T(8,128)(2,1)S(1)}, u32[]{:S(2)}, u32[]{:S(2)}) collective-permute-start(bf16[64,3584]{1,0:T(8,128)(2,1)S(1)} %pad_maximum_fusion.3), channel_id=1, source_target_pairs={{0,2},{2,0},{4,6},{6,4},{8,10},{10,8},{12,14},{14,12},{1,3},{3,1},... | collective-permute-start | bytes 1376264 | tf_op jit(solution)/shard_map/ppermute | solution.py:19
  65.5 1.1 fusion.40
  66.7 1.1 fusion.44
  67.8 4.6 %collective-permute-done.7 = bf16[64,3584]{1,0:T(8,128)(2,1)S(1)} collective-permute-done((bf16[64,3584]{1,0:T(8,128)(2,1)S(1)}, bf16[64,3584]{1,0:T(8,128)(2,1)S(1)}, u32[]{:S(2)}, u32[]{:S(2)}) %collective-permute-start.7) | collective-permute-done | bytes 458784 | tf_op jit(solution)/shard_map/ppermute | solution.py:19
  72.4 3.7 %collective-permute-start.19 = (bf16[64,3584]{1,0:T(8,128)(2,1)S(1)}, bf16[64,3584]{1,0:T(8,128)(2,1)S(1)}, u32[]{:S(2)}, u32[]{:S(2)}) collective-permute-start(bf16[64,3584]{1,0:T(8,128)(2,1)S(1)} %pad_maximum_fusion.4), channel_id=1, source_target_pairs={{0,2},{2,0},{4,6},{6,4},{8,10},{10,8},{12,14},{14,12},{1,3},{3,1},... | collective-permute-start | bytes 1376264 | tf_op jit(solution)/shard_map/ppermute | solution.py:19
  76.3 1.1 fusion.42
  77.4 5.5 %collective-permute-done.19 = bf16[64,3584]{1,0:T(8,128)(2,1)S(1)} collective-permute-done((bf16[64,3584]{1,0:T(8,128)(2,1)S(1)}, bf16[64,3584]{1,0:T(8,128)(2,1)S(1)}, u32[]{:S(2)}, u32[]{:S(2)}) %collective-permute-start.19) | collective-permute-done | bytes 458784 | tf_op jit(solution)/shard_map/ppermute | solution.py:19
  83.0 1.1 fusion.46
  84.1 1.1 fusion.43
  85.3 1.1 fusion.41
  86.6 1.1 fusion.47
  87.7 1.1 fusion.45
  94.9 4.0 %all-to-all-start.3 = ((bf16[8,64,1024]{2,1,0:T(8,128)(2,1)}), bf16[8,64,1024]{2,1,0:T(8,128)(2,1)S(1)}, u32[]{:S(2)}, u32[]{:S(2)}) async-start(bf16[8,64,1024]{2,1,0:T(8,128)(2,1)} %fusion.35), calls=%async_computation.3 | async-start | bytes 2097152 | tf_op jit(solution)/shard_map/all_to_all | solution.py:72
  104.2 5.7 %all-to-all-done.3 = bf16[8,64,1024]{2,1,0:T(8,128)(2,1)S(1)} async-done(((bf16[8,64,1024]{2,1,0:T(8,128)(2,1)}), bf16[8,64,1024]{2,1,0:T(8,128)(2,1)S(1)}, u32[]{:S(2)}, u32[]{:S(2)}) %all-to-all-start.3) | async-done | bytes 1048608 | tf_op jit(solution)/shard_map/all_to_all | solution.py:72
  110.0 4.2 %all-to-all-start = ((bf16[8,64,1024]{2,1,0:T(8,128)(2,1)}), bf16[8,64,1024]{2,1,0:T(8,128)(2,1)}, u32[]{:S(2)}, u32[]{:S(2)}) async-start(bf16[8,64,1024]{2,1,0:T(8,128)(2,1)} %fusion.27), calls=%async_computation | async-start | bytes 2097152 | tf_op jit(solution)/shard_map/all_to_all | solution.py:72
  116.1 8.5 %all-to-all-done = bf16[8,64,1024]{2,1,0:T(8,128)(2,1)} async-done(((bf16[8,64,1024]{2,1,0:T(8,128)(2,1)}), bf16[8,64,1024]{2,1,0:T(8,128)(2,1)}, u32[]{:S(2)}, u32[]{:S(2)}) %all-to-all-start) | async-done | bytes 1048608 | tf_op jit(solution)/shard_map/all_to_all | solution.py:72
  124.7 1.1 broadcast_in_dim.17
  125.8 9.7 %all-to-all-start.4 = ((bf16[8,64,1024]{2,1,0:T(8,128)(2,1)}), bf16[8,64,1024]{2,1,0:T(8,128)(2,1)S(1)}, u32[]{:S(2)}, u32[]{:S(2)}) async-start(bf16[8,64,1024]{2,1,0:T(8,128)(2,1)} %broadcast_in_dim.17), calls=%async_computation.4 | async-start | bytes 2097152 | tf_op jit(solution)/shard_map/all_to_all | solution.py:47
  135.5 1.4 convert_reduce_fusion.1
  137.7 9.6 %all-to-all-done.4 = bf16[8,64,1024]{2,1,0:T(8,128)(2,1)S(1)} async-done(((bf16[8,64,1024]{2,1,0:T(8,128)(2,1)}), bf16[8,64,1024]{2,1,0:T(8,128)(2,1)S(1)}, u32[]{:S(2)}, u32[]{:S(2)}) %all-to-all-start.4) | async-done | bytes 1048608 | tf_op jit(solution)/shard_map/all_to_all | solution.py:47
  147.4 32.7 %all_to_all.25 = bf16[8,64,1024]{2,1,0:T(8,128)(2,1)S(1)} all-to-all(bf16[8,64,1024]{2,1,0:T(8,128)(2,1)S(1)} %broadcast_in_dim.15), channel_id=1, replica_groups=mesh['x'=4,'yl'=2,'z'=4,'yh'=2,'k'=2] {'z','yh'}, dimensions={0} | all-to-all | bytes 2097152 | tf_op jit(solution)/shard_map/all_to_all | solution.py:47
  180.1 1.1 broadcast_in_dim.16
  181.2 4.6 %all-to-all-start.2 = ((bf16[8,64,1024]{2,1,0:T(8,128)(2,1)}), bf16[8,64,1024]{2,1,0:T(8,128)(2,1)S(1)}, u32[]{:S(2)}, u32[]{:S(2)}) async-start(bf16[8,64,1024]{2,1,0:T(8,128)(2,1)} %broadcast_in_dim.16), calls=%async_computation.2 | async-start | bytes 2097152 | tf_op jit(solution)/shard_map/all_to_all | solution.py:47
  185.8 2.2 %collective-permute-start.22 = (bf16[512,1024]{1,0:T(8,128)(2,1)S(1)}, bf16[512,1024]{1,0:T(8,128)(2,1)}, u32[]{:S(2)}, u32[]{:S(2)}) collective-permute-start(bf16[512,1024]{1,0:T(8,128)(2,1)S(1)} %bitcast.57), channel_id=1, source_target_pairs={{0,1},{1,0},{2,3},{3,2},{4,5},{5,4},{6,7},{7,6},{8,9},{9,8},{10,11... | collective-permute-start | bytes 3145736 | tf_op jit(solution)/shard_map/ppermute | solution.py:23
  188.1 11.5 %all-to-all-done.2 = bf16[8,64,1024]{2,1,0:T(8,128)(2,1)S(1)} async-done(((bf16[8,64,1024]{2,1,0:T(8,128)(2,1)}), bf16[8,64,1024]{2,1,0:T(8,128)(2,1)S(1)}, u32[]{:S(2)}, u32[]{:S(2)}) %all-to-all-start.2) | async-done | bytes 1048608 | tf_op jit(solution)/shard_map/all_to_all | solution.py:47
  199.8 2.8 %collective-permute-start.11 = (bf16[512,512]{1,0:T(8,128)(2,1)S(1)}, bf16[512,512]{1,0:T(8,128)(2,1)S(1)}, u32[]{:S(2)}, u32[]{:S(2)}) collective-permute-start(bf16[512,512]{1,0:T(8,128)(2,1)S(1)} %get-tuple-element.3), channel_id=1, source_target_pairs={{0,1},{1,0},{2,3},{3,2},{4,5},{5,4},{6,7},{7,6},{8,9},{9,8},{10,11... | collective-permute-start | bytes 1572872 | tf_op jit(solution)/shard_map/ppermute | solution.py:23
  202.5 1.5 collective-permute-done.11
  204.0 3.8 %fusion.10 = f32[1024,512]{1,0:T(8,128)} fusion(bf16[512,1024]{1,0:T(8,128)(2,1)} %collective-permute-done.22, bf16[512,1024]{1,0:T(8,128)(2,1)S(1)} %bitcast.58, bf16[512,512]{1,0:T(8,128)(2,1)S(1)} %collective-permute-done.11, bf16[512,512]{1,0:T(8,128)(2,1)S(1)} %get-tuple-element.2), kind=kOutput, calls=%fused_computation.16 | convolution fusion | flops 1080557568 | bytes 5242880 | tf_op jit(solution)/shard_map/dot_general | solution.py:112
  207.9 3.8 %fusion.13 = f32[1024,512]{1,0:T(8,128)} fusion(bf16[512,1024]{1,0:T(8,128)(2,1)} %collective-permute-done.10, bf16[512,1024]{1,0:T(8,128)(2,1)S(1)} %bitcast.60, bf16[512,512]{1,0:T(8,128)(2,1)S(1)} %collective-permute-done.11, bf16[512,512]{1,0:T(8,128)(2,1)S(1)} %get-tuple-element.2), kind=kOutput, calls=%fused_computation.17 | convolution fusion | flops 1080557568 | bytes 5242880 | tf_op jit(solution)/shard_map/dot_general | solution.py:111
  (86 shorter events, 15.8 us)
Async XLA Ops:
  0.6 21.5 %collective-permute-start.4 = (bf16[64,3584]{1,0:T(8,128)(2,1)}, bf16[64,3584]{1,0:T(8,128)(2,1)S(1)}, u32[]{:S(2)}, u32[]{:S(2)}) collective-permute-start(bf16[64,3584]{1,0:T(8,128)(2,1)} %param.5), channel_id=1, source_target_pairs={{0,4},{2,6},{4,8},{6,10},{8,12},{10,14},{12,0},{14,2},{1,5},{3,7},... | collective-permute-start | bytes 1376264 | tf_op jit(solution)/shard_map/ppermute | solution.py:19
  3.2 19.1 %collective-permute-start.1 = (bf16[64,3584]{1,0:T(8,128)(2,1)}, bf16[64,3584]{1,0:T(8,128)(2,1)S(1)}, u32[]{:S(2)}, u32[]{:S(2)}) collective-permute-start(bf16[64,3584]{1,0:T(8,128)(2,1)} %param.5), channel_id=1, source_target_pairs={{0,12},{2,14},{4,0},{6,2},{8,4},{10,6},{12,8},{14,10},{1,13},{3,15... | collective-permute-start | bytes 1376264 | tf_op jit(solution)/shard_map/ppermute | solution.py:19
  5.4 21.5 %collective-permute-start = (bf16[64,3584]{1,0:T(8,128)(2,1)}, bf16[64,3584]{1,0:T(8,128)(2,1)S(1)}, u32[]{:S(2)}, u32[]{:S(2)}) collective-permute-start(bf16[64,3584]{1,0:T(8,128)(2,1)} %param.5), channel_id=1, source_target_pairs={{0,2},{2,0},{4,6},{6,4},{8,10},{10,8},{12,14},{14,12},{1,3},{3,1},... | collective-permute-start | bytes 1376264 | tf_op jit(solution)/shard_map/ppermute | solution.py:19
  8.3 17.3 %collective-permute-start.16 = (bf16[64,3584]{1,0:T(8,128)(2,1)}, bf16[64,3584]{1,0:T(8,128)(2,1)S(1)}, u32[]{:S(2)}, u32[]{:S(2)}) collective-permute-start(bf16[64,3584]{1,0:T(8,128)(2,1)} %param.4), channel_id=1, source_target_pairs={{0,4},{2,6},{4,8},{6,10},{8,12},{10,14},{12,0},{14,2},{1,5},{3,7},... | collective-permute-start | bytes 1376264 | tf_op jit(solution)/shard_map/ppermute | solution.py:19
  8.3 25.7 %collective-permute-start.13 = (bf16[64,3584]{1,0:T(8,128)(2,1)}, bf16[64,3584]{1,0:T(8,128)(2,1)S(1)}, u32[]{:S(2)}, u32[]{:S(2)}) collective-permute-start(bf16[64,3584]{1,0:T(8,128)(2,1)} %param.4), channel_id=1, source_target_pairs={{0,12},{2,14},{4,0},{6,2},{8,4},{10,6},{12,8},{14,10},{1,13},{3,15... | collective-permute-start | bytes 1376264 | tf_op jit(solution)/shard_map/ppermute | solution.py:19
  12.8 6.0 %copy-start.3 = (s32[32,3584]{1,0:T(8,128)S(1)}, s32[32,3584]{1,0:T(8,128)}, u32[]{:S(2)}) copy-start(s32[32,3584]{1,0:T(8,128)} %param.7) | copy-start | bytes 1376260
  18.8 3.2 %copy-start.2 = (bf16[64,3584]{1,0:T(8,128)(2,1)S(1)}, bf16[64,3584]{1,0:T(8,128)(2,1)}, u32[]{:S(2)}) copy-start(bf16[64,3584]{1,0:T(8,128)(2,1)} %param.4) | copy-start | bytes 1376260
  18.8 3.5 %copy-start.1 = (bf16[3584,512]{1,0:T(8,128)(2,1)S(1)}, bf16[3584,512]{1,0:T(8,128)(2,1)}, u32[]{:S(2)}) copy-start(bf16[3584,512]{1,0:T(8,128)(2,1)} %param.6) | copy-start | bytes 11010052
  22.0 4.9 %copy-start.4 = (bf16[256,3584]{1,0:T(8,128)(2,1)S(1)}, bf16[256,3584]{1,0:T(8,128)(2,1)}, u32[]{:S(2)}) copy-start(bf16[256,3584]{1,0:T(8,128)(2,1)} %constant_dynamic-update-slice_fusion.3) | copy-start | bytes 5505028
  22.1 11.8 %collective-permute-start.12 = (bf16[64,3584]{1,0:T(8,128)(2,1)S(1)}, bf16[64,3584]{1,0:T(8,128)(2,1)S(1)}, u32[]{:S(2)}, u32[]{:S(2)}) collective-permute-start(bf16[64,3584]{1,0:T(8,128)(2,1)S(1)} %copy-done.2), channel_id=1, source_target_pairs={{0,2},{2,0},{4,6},{6,4},{8,10},{10,8},{12,14},{14,12},{1,3},{3,1},... | collective-permute-start | bytes 1376264 | tf_op jit(solution)/shard_map/ppermute | solution.py:19
  22.3 64.3 %collective-permute-start.15 = (bf16[3584,512]{1,0:T(8,128)(2,1)S(1)}, bf16[3584,512]{1,0:T(8,128)(2,1)S(1)}, u32[]{:S(2)}, u32[]{:S(2)}) collective-permute-start(bf16[3584,512]{1,0:T(8,128)(2,1)S(1)} %copy-done.1), channel_id=1, source_target_pairs={{0,1},{1,0},{2,3},{3,2},{4,5},{5,4},{6,7},{7,6},{8,9},{9,8},{10,11... | collective-permute-start | bytes 11010056 | tf_op jit(solution)/shard_map/ppermute | solution.py:23
  25.6 58.5 %collective-permute-start.3 = (bf16[3584,512]{0,1:T(8,128)(2,1)S(1)}, bf16[3584,512]{0,1:T(8,128)(2,1)S(1)}, u32[]{:S(2)}, u32[]{:S(2)}) collective-permute-start(bf16[3584,512]{0,1:T(8,128)(2,1)S(1)} %bitcast_select_fusion), channel_id=1, source_target_pairs={{0,1},{1,0},{2,3},{3,2},{4,5},{5,4},{6,7},{7,6},{8,9},{9,8},{10,11... | collective-permute-start | bytes 11010056 | tf_op jit(solution)/shard_map/ppermute | solution.py:23
  26.8 8.7 %collective-permute-start.5 = (bf16[32,3584]{1,0:T(8,128)(2,1)S(1)}, bf16[32,3584]{1,0:T(8,128)(2,1)S(1)}, u32[]{:S(2)}, u32[]{:S(2)}) collective-permute-start(bf16[32,3584]{1,0:T(8,128)(2,1)S(1)} %slice.32), channel_id=1, source_target_pairs={{0,4},{2,6},{4,8},{6,10},{8,12},{10,14},{12,0},{14,2},{1,5},{3,7},... | collective-permute-start | bytes 688136 | tf_op jit(solution)/shard_map/ppermute | solution.py:19
  33.9 4.9 %collective-permute-start.6 = (bf16[32,3584]{1,0:T(8,128)(2,1)S(1)}, bf16[32,3584]{1,0:T(8,128)(2,1)S(1)}, u32[]{:S(2)}, u32[]{:S(2)}) collective-permute-start(bf16[32,3584]{1,0:T(8,128)(2,1)S(1)} %slice.33), channel_id=1, source_target_pairs={{0,12},{2,14},{4,0},{6,2},{8,4},{10,6},{12,8},{14,10},{1,13},{3,15... | collective-permute-start | bytes 688136 | tf_op jit(solution)/shard_map/ppermute | solution.py:19
  33.9 6.2 %collective-permute-start.17 = (bf16[32,3584]{1,0:T(8,128)(2,1)S(1)}, bf16[32,3584]{1,0:T(8,128)(2,1)S(1)}, u32[]{:S(2)}, u32[]{:S(2)}) collective-permute-start(bf16[32,3584]{1,0:T(8,128)(2,1)S(1)} %slice.36), channel_id=1, source_target_pairs={{0,4},{2,6},{4,8},{6,10},{8,12},{10,14},{12,0},{14,2},{1,5},{3,7},... | collective-permute-start | bytes 688136 | tf_op jit(solution)/shard_map/ppermute | solution.py:19
  35.5 7.6 %collective-permute-start.18 = (bf16[32,3584]{1,0:T(8,128)(2,1)S(1)}, bf16[32,3584]{1,0:T(8,128)(2,1)S(1)}, u32[]{:S(2)}, u32[]{:S(2)}) collective-permute-start(bf16[32,3584]{1,0:T(8,128)(2,1)S(1)} %slice.37), channel_id=1, source_target_pairs={{0,12},{2,14},{4,0},{6,2},{8,4},{10,6},{12,8},{14,10},{1,13},{3,15... | collective-permute-start | bytes 688136 | tf_op jit(solution)/shard_map/ppermute | solution.py:19
  38.8 37.4 %collective-permute-start.8 = (bf16[64,3584]{1,0:T(8,128)(2,1)S(1)}, bf16[64,3584]{1,0:T(8,128)(2,1)S(1)}, u32[]{:S(2)}, u32[]{:S(2)}) collective-permute-start(bf16[64,3584]{1,0:T(8,128)(2,1)S(1)} %collective-permute-done), channel_id=1, source_target_pairs={{0,4},{2,6},{4,8},{6,10},{8,12},{10,14},{12,0},{14,2},{1,5},{3,7},... | collective-permute-start | bytes 1376264 | tf_op jit(solution)/shard_map/ppermute | solution.py:19
  40.1 12.9 %collective-permute-start.2 = (bf16[64,3584]{1,0:T(8,128)(2,1)S(1)}, bf16[64,3584]{1,0:T(8,128)(2,1)S(1)}, u32[]{:S(2)}, u32[]{:S(2)}) collective-permute-start(bf16[64,3584]{1,0:T(8,128)(2,1)S(1)} %collective-permute-done), channel_id=1, source_target_pairs={{0,12},{2,14},{4,0},{6,2},{8,4},{10,6},{12,8},{14,10},{1,13},{3,15... | collective-permute-start | bytes 1376264 | tf_op jit(solution)/shard_map/ppermute | solution.py:19
  43.2 39.7 %collective-permute-start.20 = (bf16[64,3584]{1,0:T(8,128)(2,1)S(1)}, bf16[64,3584]{1,0:T(8,128)(2,1)S(1)}, u32[]{:S(2)}, u32[]{:S(2)}) collective-permute-start(bf16[64,3584]{1,0:T(8,128)(2,1)S(1)} %collective-permute-done.12), channel_id=1, source_target_pairs={{0,4},{2,6},{4,8},{6,10},{8,12},{10,14},{12,0},{14,2},{1,5},{3,7},... | collective-permute-start | bytes 1376264 | tf_op jit(solution)/shard_map/ppermute | solution.py:19
  53.0 9.0 %collective-permute-start.14 = (bf16[64,3584]{1,0:T(8,128)(2,1)S(1)}, bf16[64,3584]{1,0:T(8,128)(2,1)S(1)}, u32[]{:S(2)}, u32[]{:S(2)}) collective-permute-start(bf16[64,3584]{1,0:T(8,128)(2,1)S(1)} %collective-permute-done.12), channel_id=1, source_target_pairs={{0,12},{2,14},{4,0},{6,2},{8,4},{10,6},{12,8},{14,10},{1,13},{3,15... | collective-permute-start | bytes 1376264 | tf_op jit(solution)/shard_map/ppermute | solution.py:19
  62.0 10.4 %collective-permute-start.7 = (bf16[64,3584]{1,0:T(8,128)(2,1)S(1)}, bf16[64,3584]{1,0:T(8,128)(2,1)S(1)}, u32[]{:S(2)}, u32[]{:S(2)}) collective-permute-start(bf16[64,3584]{1,0:T(8,128)(2,1)S(1)} %pad_maximum_fusion.3), channel_id=1, source_target_pairs={{0,2},{2,0},{4,6},{6,4},{8,10},{10,8},{12,14},{14,12},{1,3},{3,1},... | collective-permute-start | bytes 1376264 | tf_op jit(solution)/shard_map/ppermute | solution.py:19
  72.4 10.4 %collective-permute-start.19 = (bf16[64,3584]{1,0:T(8,128)(2,1)S(1)}, bf16[64,3584]{1,0:T(8,128)(2,1)S(1)}, u32[]{:S(2)}, u32[]{:S(2)}) collective-permute-start(bf16[64,3584]{1,0:T(8,128)(2,1)S(1)} %pad_maximum_fusion.4), channel_id=1, source_target_pairs={{0,2},{2,0},{4,6},{6,4},{8,10},{10,8},{12,14},{14,12},{1,3},{3,1},... | collective-permute-start | bytes 1376264 | tf_op jit(solution)/shard_map/ppermute | solution.py:19
  89.4 4.8 %copy-start = (f32[8,64,1024]{2,1,0:T(8,128)}, f32[8,64,1024]{2,1,0:T(8,128)S(1)}, u32[]{:S(2)}) copy-start(f32[8,64,1024]{2,1,0:T(8,128)S(1)} %sub.40) | copy-start | bytes 6291460
  94.9 15.1 %all-to-all-start.3 = ((bf16[8,64,1024]{2,1,0:T(8,128)(2,1)}), bf16[8,64,1024]{2,1,0:T(8,128)(2,1)S(1)}, u32[]{:S(2)}, u32[]{:S(2)}) async-start(bf16[8,64,1024]{2,1,0:T(8,128)(2,1)} %fusion.35), calls=%async_computation.3 | async-start | bytes 2097152 | tf_op jit(solution)/shard_map/all_to_all | solution.py:72
  110.0 14.7 %all-to-all-start = ((bf16[8,64,1024]{2,1,0:T(8,128)(2,1)}), bf16[8,64,1024]{2,1,0:T(8,128)(2,1)}, u32[]{:S(2)}, u32[]{:S(2)}) async-start(bf16[8,64,1024]{2,1,0:T(8,128)(2,1)} %fusion.27), calls=%async_computation | async-start | bytes 2097152 | tf_op jit(solution)/shard_map/all_to_all | solution.py:72
  115.5 9.2 %collective-permute-start.21 = (bf16[64,1024]{1,0:T(8,128)(2,1)S(1)}, bf16[64,1024]{1,0:T(8,128)(2,1)S(1)}, u32[]{:S(2)}, u32[]{:S(2)}) collective-permute-start(bf16[64,1024]{1,0:T(8,128)(2,1)S(1)} %fusion.17), channel_id=1, source_target_pairs={{0,0},{1,1},{2,16},{3,17},{4,32},{5,33},{6,48},{7,49},{8,64},{9,65... | collective-permute-start | bytes 393224 | tf_op jit(solution)/shard_map/ppermute | solution.py:42
  125.8 21.5 %all-to-all-start.4 = ((bf16[8,64,1024]{2,1,0:T(8,128)(2,1)}), bf16[8,64,1024]{2,1,0:T(8,128)(2,1)S(1)}, u32[]{:S(2)}, u32[]{:S(2)}) async-start(bf16[8,64,1024]{2,1,0:T(8,128)(2,1)} %broadcast_in_dim.17), calls=%async_computation.4 | async-start | bytes 2097152 | tf_op jit(solution)/shard_map/all_to_all | solution.py:47
  137.0 0.7 collective-permute-start.9
  181.2 18.4 %all-to-all-start.2 = ((bf16[8,64,1024]{2,1,0:T(8,128)(2,1)}), bf16[8,64,1024]{2,1,0:T(8,128)(2,1)S(1)}, u32[]{:S(2)}, u32[]{:S(2)}) async-start(bf16[8,64,1024]{2,1,0:T(8,128)(2,1)} %broadcast_in_dim.16), calls=%async_computation.2 | async-start | bytes 2097152 | tf_op jit(solution)/shard_map/all_to_all | solution.py:47
  185.8 18.3 %collective-permute-start.22 = (bf16[512,1024]{1,0:T(8,128)(2,1)S(1)}, bf16[512,1024]{1,0:T(8,128)(2,1)}, u32[]{:S(2)}, u32[]{:S(2)}) collective-permute-start(bf16[512,1024]{1,0:T(8,128)(2,1)S(1)} %bitcast.57), channel_id=1, source_target_pairs={{0,1},{1,0},{2,3},{3,2},{4,5},{5,4},{6,7},{7,6},{8,9},{9,8},{10,11... | collective-permute-start | bytes 3145736 | tf_op jit(solution)/shard_map/ppermute | solution.py:23
  188.0 19.9 %collective-permute-start.10 = (bf16[512,1024]{1,0:T(8,128)(2,1)S(1)}, bf16[512,1024]{1,0:T(8,128)(2,1)}, u32[]{:S(2)}, u32[]{:S(2)}) collective-permute-start(bf16[512,1024]{1,0:T(8,128)(2,1)S(1)} %bitcast.59), channel_id=1, source_target_pairs={{0,1},{1,0},{2,3},{3,2},{4,5},{5,4},{6,7},{7,6},{8,9},{9,8},{10,11... | collective-permute-start | bytes 3145736 | tf_op jit(solution)/shard_map/ppermute | solution.py:23
  199.8 4.3 %collective-permute-start.11 = (bf16[512,512]{1,0:T(8,128)(2,1)S(1)}, bf16[512,512]{1,0:T(8,128)(2,1)S(1)}, u32[]{:S(2)}, u32[]{:S(2)}) collective-permute-start(bf16[512,512]{1,0:T(8,128)(2,1)S(1)} %get-tuple-element.3), channel_id=1, source_target_pairs={{0,1},{1,0},{2,3},{3,2},{4,5},{5,4},{6,7},{7,6},{8,9},{9,8},{10,11... | collective-permute-start | bytes 1572872 | tf_op jit(solution)/shard_map/ppermute | solution.py:23

commit v2 on v1

v2 whole, which is shorter than its diff:
```python
import functools

import jax
import jax.numpy as jnp
from jax import lax
from jax.experimental import pallas as pl
from jax.experimental.pallas import tpu as pltpu
from jax.sharding import Mesh
from jax.sharding import PartitionSpec as P

ROW = ("x", "yl")
SIDE = ("z", "yh")
COL = ("z", "yh", "k")
BF = jnp.bfloat16
F32 = jnp.float32


PLACES = ((0, 0), (0, 1), (3, 0), (1, 0), (3, 1), (1, 1), (2, 0), (2, 1))


def step(a, dz, dy, axes=SIDE):
    nz, ny = lax.axis_size(axes[0]), lax.axis_size(axes[1])
    pairs = [
        (z * ny + y, ((z + dz) % nz) * ny + (y + dy) % ny) for z in range(nz) for y in range(ny)
    ]
    return lax.ppermute(a, axes, pairs)


def swap(a):
    return lax.ppermute(a, "k", [(0, 1), (1, 0)])


def after(a, *done):
    return lax.optimization_barrier((a,) + done)[0]


def transposed(a):
    pairs = []
    for r in range(8):
        for c in range(8):
            for k in range(2):
                pairs.append(((r * 8 + c) * 2 + k, (c * 8 + r) * 2 + k))
    return lax.ppermute(a, ROW + COL, pairs)


def spread(a, axes):
    n = lax.axis_size(axes)
    return lax.all_to_all(jnp.broadcast_to(a, (n,) + a.shape), axes, 0, 0, tiled=True)


def pruned(weight, words):
    n = weight.shape[1]
    rows = words.shape[0]
    halves = jnp.concatenate([words & 255, jnp.right_shift(words, 8)], 0).astype(BF)
    column = jnp.arange(n)
    source = column // 16 + rows * (column % 16 // 8)
    ones = (jnp.arange(2 * rows)[:, None] == source[None, :]).astype(BF)
    dims = (((0,), (0,)), ((), ()))
    byte = lax.dot_general(halves, ones, dims, preferred_element_type=F32).astype(jnp.int32)
    flag = jnp.right_shift(byte, (column % 8)[None, :]) & 1
    return jnp.where(flag == 1, weight, jnp.zeros_like(weight))


def dots(blocks, weights):
    a = jnp.concatenate(blocks, 0)
    outs = [jnp.dot(a, w, preferred_element_type=F32) for w in weights]
    return [o.reshape(len(blocks), -1, o.shape[1]) for o in outs]


def joined(first, second):
    return jnp.concatenate([jnp.concatenate(h, 2) for h in (first, second)], 0)


def place_kernel(at_ref, blocks, out):
    for i in range(8):
        out[at_ref[i]] = blocks[i]


def placed(blocks, at):
    vmem = pl.BlockSpec(memory_space=pltpu.VMEM)
    return pl.pallas_call(
        place_kernel,
        in_specs=[pl.BlockSpec(memory_space=pltpu.SMEM), vmem],
        out_specs=vmem,
        out_shape=jax.ShapeDtypeStruct(blocks.shape, BF),
        compiler_params=pltpu.CompilerParams(vmem_limit_bytes=4 * 1024 * 1024),
        name="placed",
    )(jnp.stack(at).astype(jnp.int32), blocks)


def summed(sent, partial):
    own = lax.dynamic_index_in_dim(partial, lax.axis_index(ROW), 0, False)
    came = lax.all_to_all(sent, ROW, 0, 0, tiled=True)
    total = jnp.sum(came.astype(F32), 0) + (own - own.astype(BF).astype(F32))
    half = total.shape[1] // 2
    crossed = jnp.concatenate([total[:, half:], total[:, :half]], 1)
    return jnp.where(lax.axis_index("k") == 0, total, crossed).astype(BF)


def lookup(table, at):
    out = 0
    for i, t in enumerate(table):
        out = out + jnp.where(at == i, t, 0)
    return out


def columns(blocks):
    x, yl, z, yh = (lax.axis_index(a) for a in ROW + SIDE)
    number = [PLACES.index((i // 2, i % 2)) for i in range(8)]
    at = []
    for a, b in PLACES:
        at.append(lookup(number, (z - x + a + 4) % 4 * 2 + (yh - yl + b + 2) % 2))
    every = placed(blocks, at)
    k = lax.axis_index("k")
    half = every.shape[2] // 2
    mine = lax.dynamic_slice_in_dim(every, k * half, half, 2)
    others = lax.dynamic_slice_in_dim(every, (1 - k) * half, half, 2)
    return mine, swap(others)


def product(rows, cols):
    dims = (((0, 1), (0, 1)), ((), ()))
    return lax.dot_general(rows, cols, dims, preferred_element_type=F32)


def local(dense_in, pruned_in, weight, keep_bits):
    tokens = dense_in.shape[0] * lax.axis_size(COL)
    n = dense_in.shape[0]
    h = n // 2
    p_side, p_up, p_down = step(pruned_in, 0, 1), step(pruned_in, 1, 0), step(pruned_in, 3, 0)
    weight_o = swap(weight)
    pruned_w = pruned(weight, keep_bits)
    p_side, p_up, p_down, pruned_w = lax.optimization_barrier((p_side, p_up, p_down, pruned_w))
    pruned_o = swap(pruned_w)
    p_up2 = step(jnp.concatenate([p_side, p_up[: n // 2]], 0), 1, 0)
    p_down2 = step(jnp.concatenate([p_side, p_down[n // 2 :]], 0), 3, 0)
    d_side = step(after(dense_in, p_side), 0, 1)
    p_up2, p_down2, d_side = lax.optimization_barrier((p_up2, p_down2, d_side))
    p_across = jnp.concatenate([p_up2[n:], p_down2[n:]], 0)
    p_side_across = step(p_across, 0, 1)
    d_pair = jnp.concatenate([dense_in, d_side], 0)
    d_up, d_down = step(d_pair, 1, 0), step(d_pair, 3, 0)
    pruned_ws, dense_ws = (pruned_w, pruned_o), (weight, weight_o)
    p_first = dots([pruned_in, p_side, p_up, p_down], pruned_ws)
    p_second = dots([p_up2[:n], p_down2[:n], p_across, p_side_across], pruned_ws)
    part_p = joined(p_first, p_second)
    sent_p = part_p.astype(BF)
    d_up, d_down, part_p, sent_p = lax.optimization_barrier((d_up, d_down, part_p, sent_p))
    p = summed(sent_p, part_p)
    d_across, d_side_across = step(d_up[:n], 1, 0), step(d_down[n:], 3, 0)
    d_first = dots([dense_in, d_side, d_up[:n], d_down[:n]], dense_ws)
    d_across, d_side_across, p, *d_first = lax.optimization_barrier((d_across, d_side_across, p, *d_first))
    d_second = dots([d_up[n:], d_down[n:], d_across, d_side_across], dense_ws)
    part_d = joined(d_first, d_second) - part_p
    sent_d = part_d.astype(BF)
    p, part_d, sent_d = lax.optimization_barrier((p, part_d, sent_d))
    d = summed(sent_d, part_d)
    t_p = transposed(p)
    d, p, t_p = lax.optimization_barrier((d, p, t_p))
    t_d = transposed(d)
    every = spread(p, ROW)
    t_d, every = lax.optimization_barrier((t_d, every))
    rows = spread(jnp.concatenate([t_p, t_d], 0), SIDE)
    cols = columns(every)
    others = swap(rows)
    gram_tile = (product(rows[:, :n], cols[0]) + product(others[:, :n], cols[1])) / tokens
    cross_tile = (product(rows[:, n:], cols[0]) + product(others[:, n:], cols[1])) / tokens
    return (gram_tile, cross_tile)


def solution(mesh):
    split = Mesh(mesh.devices.reshape(4, 2, 4, 2, 2), ROW + COL)
    in_specs = (P(COL, ROW), P(COL, ROW), P(ROW, COL), P(COL, ROW))
    out_specs = (P(ROW, COL), P(ROW, COL))
    return jax.shard_map(local, mesh=split, in_specs=in_specs, out_specs=out_specs, check_vma=False)
```

time: 212 us -> 172 us (0.81)
  waiting for transfers between devices: 78.2 us -> 47.6 us
  matrix products: 16.6 us -> 32 us
  local copies, waits for them, and re-layouts: 21.6 us -> 8.64 us
  blocking collectives: 32.7 us -> 26.2 us
  starting transfers between devices: 54.8 us -> 48.6 us
    ppermute x16 -> x11, waiting for transfers between devices: 41.3 us -> 25.3 us  [step(): return lax.ppermute(a, axes, pairs)]
    dot_general x10 -> x13, matrix products: 16.6 us -> 32 us  [the longest x8 19.8 us: dots(): outs = [jnp.dot(a, w, preferred_element_type=F32) for w in weights]]
    unnamed x39 -> x22, local copies, waits for them, and re-layouts: 17.6 us -> 2.72 us
    all_to_all x2 -> x1, waiting for transfers between devices: 21.2 us -> 9.66 us  [spread(): lax.all_to_all(jnp.broadcast_to(a, (n,) + a.shape), axes, 0, 0, tiled=True)]
    all_to_all x2 -> x1, starting transfers between devices: 14.3 us -> 6.58 us  [spread(): lax.all_to_all(jnp.broadcast_to(a, (n,) + a.shape), axes, 0, 0, tiled=True)]
    all_to_all x1, blocking collectives: 32.7 us -> 26.2 us  [spread(): lax.all_to_all(jnp.broadcast_to(a, (n,) + a.shape), axes, 0, 0, tiled=True)]
    ppermute x5 -> x4, starting transfers between devices: 8.46 us -> 14.5 us  [swap(): return lax.ppermute(a, 'k', [(0, 1), (1, 0)])]
    ppermute x16 -> x11, starting transfers between devices: 22.4 us -> 16.6 us  [step(): return lax.ppermute(a, axes, pairs)]
  transfers between devices with their start and end apart: 27 -> 20, of which waited for: 14 -> 8; matrix products, arithmetic and copies ran while one was open for 14% -> 17% of each run, Pallas kernels for 0% -> 0%
where the time goes in v2:
time: 172 us; the launch traced here: 171 us
  starting transfers between devices  48.6 us (28%)
  waiting for transfers between devices  47.6 us (28%)
  matrix products  32 us (19%)
  blocking collectives  26.2 us (15%)
  local copies, waits for them, and re-layouts  8.64 us (5%)
  other arithmetic  6.17 us (4%)
    all_to_all x1, blocking collectives, spread(): lax.all_to_all(jnp.broadcast_to(a, (n,) + a.shape), axes, 0, 0, tiled=True)  26.2 us
    ppermute x11, waiting for transfers between devices, step(): return lax.ppermute(a, axes, pairs)  25.3 us
    dot_general x8, matrix products, dots(): outs = [jnp.dot(a, w, preferred_element_type=F32) for w in weights]  19.8 us
    ppermute x11, starting transfers between devices, step(): return lax.ppermute(a, axes, pairs)  16.6 us
    ppermute x4, starting transfers between devices, swap(): return lax.ppermute(a, 'k', [(0, 1), (1, 0)])  14.5 us
    all_to_all x2, waiting for transfers between devices, summed(): came = lax.all_to_all(sent, ROW, 0, 0, tiled=True)  10.5 us
    all_to_all x1, waiting for transfers between devices, spread(): lax.all_to_all(jnp.broadcast_to(a, (n,) + a.shape), axes, 0, 0, tiled=True)  9.66 us
    all_to_all x2, starting transfers between devices, summed(): came = lax.all_to_all(sent, ROW, 0, 0, tiled=True)  9.54 us
  transfers between devices with their start and end apart: 20, of which 8 were waited for; matrix products, arithmetic and copies ran while one was open for 17% of the time, Pallas kernels for 0%

profile of v2, /device:TPU:1, one launch (start us, length us, event | category | flops | bytes accessed | tf_op | source)
XLA Modules:
  0.0 170.9 jit_solution(3833793717369066818)
XLA Ops:
  0.6 3.8 %collective-permute-start = (bf16[64,3584]{1,0:T(8,128)(2,1)}, bf16[64,3584]{1,0:T(8,128)(2,1)S(1)}, u32[]{:S(2)}, u32[]{:S(2)}) collective-permute-start(bf16[64,3584]{1,0:T(8,128)(2,1)} %param.5), channel_id=1, source_target_pairs={{0,2},{2,0},{4,6},{6,4},{8,10},{10,8},{12,14},{14,12},{1,3},{3,1},... | collective-permute-start | bytes 1376264 | tf_op jit(solution)/shard_map/ppermute | solution.py:26
  4.5 1.6 collective-permute-start.1
  6.1 2.1 %collective-permute-start.2 = (bf16[64,3584]{1,0:T(8,128)(2,1)}, bf16[64,3584]{1,0:T(8,128)(2,1)S(1)}, u32[]{:S(2)}, u32[]{:S(2)}) collective-permute-start(bf16[64,3584]{1,0:T(8,128)(2,1)} %param.5), channel_id=1, source_target_pairs={{0,12},{2,14},{4,0},{6,2},{8,4},{10,6},{12,8},{14,10},{1,13},{3,15... | collective-permute-start | bytes 1376264 | tf_op jit(solution)/shard_map/ppermute | solution.py:26
  8.2 1.2 collective-permute-start.12
  9.5 1.8 %constant_dynamic-update-slice_fusion.5 = bf16[256,3584]{1,0:T(8,128)(2,1)} fusion(bf16[64,3584]{1,0:T(8,128)(2,1)} %param.5), kind=kLoop, calls=%fused_computation.52 | loop fusion | bytes 917504
  11.3 1.1 and_convert_fusion
  12.4 4.1 %fusion = bf16[3584,512]{1,0:T(8,128)(2,1)S(1)} fusion(bf16[3584,512]{1,0:T(8,128)(2,1)} %param.6, s32[512]{0:T(512)S(1)} %get-tuple-element.70, bf16[32,3584]{1,0:T(8,128)(2,1)S(1)} %get-tuple-element.65, bf16[32,3584]{1,0:T(8,128)(2,1)S(1)} %get-tuple-element.64, s32[512]{0:T(512)S(1)} %get-tuple-element.71), kind=kOutput, calls=%fused_computation.1 | convolution fusion | flops 245006336 | bytes 7802880 | tf_op jit(solution)/shard_map/dot_general | solution.py:59
  16.5 1.8 %collective-permute-done.1 = bf16[64,3584]{1,0:T(8,128)(2,1)S(1)} collective-permute-done((bf16[64,3584]{1,0:T(8,128)(2,1)}, bf16[64,3584]{1,0:T(8,128)(2,1)S(1)}, u32[]{:S(2)}, u32[]{:S(2)}) %collective-permute-start.1) | collective-permute-done | bytes 458784 | tf_op jit(solution)/shard_map/ppermute | solution.py:26
  18.9 2.3 %collective-permute-start.4 = (bf16[96,3584]{1,0:T(8,128)(2,1)S(1)}, bf16[96,3584]{1,0:T(8,128)(2,1)S(1)}, u32[]{:S(2)}, u32[]{:S(2)}) collective-permute-start(bf16[96,3584]{1,0:T(8,128)(2,1)S(1)} %get-tuple-element.62), channel_id=1, source_target_pairs={{0,12},{2,14},{4,0},{6,2},{8,4},{10,6},{12,8},{14,10},{1,13},{3,15... | collective-permute-start | bytes 2064392 | tf_op jit(solution)/shard_map/ppermute | solution.py:26
  21.6 2.1 %collective-permute-start.8 = (bf16[3584,512]{1,0:T(8,128)(2,1)S(1)}, bf16[3584,512]{1,0:T(8,128)(2,1)S(1)}, u32[]{:S(2)}, u32[]{:S(2)}) collective-permute-start(bf16[3584,512]{1,0:T(8,128)(2,1)S(1)} %fusion), channel_id=1, source_target_pairs={{0,1},{1,0},{2,3},{3,2},{4,5},{5,4},{6,7},{7,6},{8,9},{9,8},{10,11... | collective-permute-start | bytes 11010056 | tf_op jit(solution)/shard_map/ppermute | solution.py:30
  23.8 1.1 fusion.52
  25.0 7.7 %collective-permute-done.5 = bf16[64,3584]{1,0:T(8,128)(2,1)S(1)} collective-permute-done((bf16[64,3584]{1,0:T(8,128)(2,1)S(1)}, bf16[64,3584]{1,0:T(8,128)(2,1)S(1)}, u32[]{:S(2)}, u32[]{:S(2)}) %collective-permute-start.5) | collective-permute-done | bytes 458784 | tf_op jit(solution)/shard_map/ppermute | solution.py:26
  32.7 2.5 %collective-permute-done.3 = bf16[96,3584]{1,0:T(8,128)(2,1)S(1)} collective-permute-done((bf16[96,3584]{1,0:T(8,128)(2,1)S(1)}, bf16[96,3584]{1,0:T(8,128)(2,1)S(1)}, u32[]{:S(2)}, u32[]{:S(2)}) %collective-permute-start.3) | collective-permute-done | bytes 688160 | tf_op jit(solution)/shard_map/ppermute | solution.py:26
  35.4 0.6 collective-permute-start.9
  36.0 0.6 collective-permute-start.6
  36.5 2.2 %collective-permute-start.7 = (bf16[128,3584]{1,0:T(8,128)(2,1)S(1)}, bf16[128,3584]{1,0:T(8,128)(2,1)}, u32[]{:S(2)}, u32[]{:S(2)}) collective-permute-start(bf16[128,3584]{1,0:T(8,128)(2,1)S(1)} %constant_dynamic-update-slice_fusion), channel_id=1, source_target_pairs={{0,12},{2,14},{4,0},{6,2},{8,4},{10,6},{12,8},{14,10},{1,13},{3,15... | collective-permute-start | bytes 2752520 | tf_op jit(solution)/shard_map/ppermute | solution.py:26
  38.7 7.8 %collective-permute-done.9 = bf16[64,3584]{1,0:T(8,128)(2,1)S(1)} collective-permute-done((bf16[64,3584]{1,0:T(8,128)(2,1)S(1)}, bf16[64,3584]{1,0:T(8,128)(2,1)S(1)}, u32[]{:S(2)}, u32[]{:S(2)}) %collective-permute-start.9) | collective-permute-done | bytes 458784 | tf_op jit(solution)/shard_map/ppermute | solution.py:26
  46.6 1.1 fusion.54
  47.7 1.1 fusion.55
  48.8 1.1 fusion.53
  49.9 1.1 fusion.44
  51.2 5.5 %collective-permute-done.6 = bf16[128,3584]{1,0:T(8,128)(2,1)} collective-permute-done((bf16[128,3584]{1,0:T(8,128)(2,1)S(1)}, bf16[128,3584]{1,0:T(8,128)(2,1)}, u32[]{:S(2)}, u32[]{:S(2)}) %collective-permute-start.6) | collective-permute-done | bytes 917536 | tf_op jit(solution)/shard_map/ppermute | solution.py:26
  56.7 4.4 %all-to-all-start = ((bf16[8,64,1024]{2,1,0:T(8,128)(2,1)}), bf16[8,64,1024]{2,1,0:T(8,128)(2,1)S(1)}, u32[]{:S(2)}, u32[]{:S(2)}) async-start(bf16[8,64,1024]{2,1,0:T(8,128)(2,1)} %fusion.44), calls=%async_computation | async-start | bytes 2097152 | tf_op jit(solution)/shard_map/all_to_all | solution.py:93
  61.1 2.2 %fusion.46 = (bf16[64,3584]{1,0:T(8,128)(2,1)}, bf16[64,3584]{1,0:T(8,128)(2,1)}) fusion(bf16[128,3584]{1,0:T(8,128)(2,1)} %collective-permute-done.6), kind=kLoop, calls=%fused_computation.91 | loop fusion | bytes 1835008 | tf_op jit(solution)/shard_map/slice | solution.py:153
  63.5 2.0 %fusion.47 = (bf16[64,3584]{1,0:T(8,128)(2,1)S(1)}, bf16[64,3584]{1,0:T(8,128)(2,1)}) fusion(bf16[128,3584]{1,0:T(8,128)(2,1)} %collective-permute-done.7), kind=kLoop, calls=%fused_computation.92 | loop fusion | bytes 1835008 | tf_op jit(solution)/shard_map/slice | solution.py:151
  65.4 2.6 %collective-permute-start.11 = (bf16[64,3584]{1,0:T(8,128)(2,1)}, bf16[64,3584]{1,0:T(8,128)(2,1)}, u32[]{:S(2)}, u32[]{:S(2)}) collective-permute-start(bf16[64,3584]{1,0:T(8,128)(2,1)} %get-tuple-element.57), channel_id=1, source_target_pairs={{0,12},{2,14},{4,0},{6,2},{8,4},{10,6},{12,8},{14,10},{1,13},{3,15... | collective-permute-start | bytes 1376264 | tf_op jit(solution)/shard_map/ppermute | solution.py:26
  68.0 4.1 %fusion.17 = f32[256,512]{1,0:T(8,128)} fusion(bf16[3584,512]{1,0:T(8,128)(2,1)} %param.6, bf16[64,3584]{1,0:T(8,128)(2,1)S(1)} %get-tuple-element.56, bf16[64,3584]{1,0:T(8,128)(2,1)} %get-tuple-element.55, bf16[64,3584]{1,0:T(8,128)(2,1)S(1)} %copy-done.6, bf16[64,3584]{1,0:T(8,128)(2,1)S(1)} %copy-done.4), kind=kOutput, calls=%fused_computation.33 | convolution fusion | flops 946864128 | bytes 6029312 | tf_op jit(solution)/shard_map/dot_general | solution.py:66
  72.1 4.1 %fusion.16 = f32[256,512]{1,0:T(8,128)} fusion(bf16[3584,512]{1,0:T(8,128)(2,1)} %collective-permute-done.12, bf16[64,3584]{1,0:T(8,128)(2,1)S(1)} %get-tuple-element.56, bf16[64,3584]{1,0:T(8,128)(2,1)} %get-tuple-element.55, bf16[64,3584]{1,0:T(8,128)(2,1)S(1)} %copy-done.6, bf16[64,3584]{1,0:T(8,128)(2,1)S(1)} %copy-done.4), kind=kOutput, calls=%fused_computation.32 | convolution fusion | flops 946864128 | bytes 6029312 | tf_op jit(solution)/shard_map/dot_general | solution.py:66
  76.5 0.7 copy-done.2
  77.2 3.6 %fusion.15 = f32[256,512]{1,0:T(8,128)S(1)} fusion(bf16[3584,512]{1,0:T(8,128)(2,1)} %param.6, bf16[64,3584]{1,0:T(8,128)(2,1)} %collective-permute-done.11, bf16[64,3584]{1,0:T(8,128)(2,1)} %collective-permute-done.10, bf16[64,3584]{1,0:T(8,128)(2,1)} %get-tuple-element.57, bf16[64,3584]{1,0:T(8,128)(2,1)S(1)} %copy-done.2), kind=kOutput, calls=%fused_computation.31 | convolution fusion | flops 946864128 | bytes 6029312 | tf_op jit(solution)/shard_map/dot_general | solution.py:66
  80.8 3.6 %fusion.14 = f32[256,512]{1,0:T(8,128)S(1)} fusion(bf16[3584,512]{1,0:T(8,128)(2,1)} %collective-permute-done.12, bf16[64,3584]{1,0:T(8,128)(2,1)} %collective-permute-done.11, bf16[64,3584]{1,0:T(8,128)(2,1)} %collective-permute-done.10, bf16[64,3584]{1,0:T(8,128)(2,1)} %get-tuple-element.57, bf16[64,3584]{1,0:T(8,128)(2,1)S(1)} %copy-done.2), kind=kOutput, calls=%fused_computation.30 | convolution fusion | flops 946864128 | bytes 6029312 | tf_op jit(solution)/shard_map/dot_general | solution.py:66
  84.5 2.2 %fusion.45 = (bf16[8,64,1024]{2,1,0:T(8,128)(2,1)}, f32[8,64,1024]{2,1,0:T(8,128)}) fusion(f32[8,64,1024]{2,1,0:T(8,128)S(1)} %maximum_maximum_fusion, f32[4,64,512]{2,1,0:T(8,128)S(1)} %bitcast.67, f32[4,64,512]{2,1,0:T(8,128)S(1)} %bitcast.66, f32[4,64,512]{2,1,0:T(8,128)S(1)} %bitcast.65, f32[4,64,512]{2,1,0:T(8,128)S(1)} %bitcast.64), kind=kLoop, calls=%fused_computation.90 | loop fusion | flops 2621440 | bytes 7340032 | tf_op jit(solution)/shard_map/convert_element_type | solution.py:155
  86.7 5.1 %all-to-all-start.1 = ((bf16[8,64,1024]{2,1,0:T(8,128)(2,1)}), bf16[8,64,1024]{2,1,0:T(8,128)(2,1)S(1)}, u32[]{:S(2)}, u32[]{:S(2)}) async-start(bf16[8,64,1024]{2,1,0:T(8,128)(2,1)} %get-tuple-element.44), calls=%async_computation.1 | async-start | bytes 2097152 | tf_op jit(solution)/shard_map/all_to_all | solution.py:93
  91.8 0.7 collective-permute-start.13
  92.5 10.5 %all-to-all-done.1 = bf16[8,64,1024]{2,1,0:T(8,128)(2,1)S(1)} async-done(((bf16[8,64,1024]{2,1,0:T(8,128)(2,1)}), bf16[8,64,1024]{2,1,0:T(8,128)(2,1)S(1)}, u32[]{:S(2)}, u32[]{:S(2)}) %all-to-all-start.1) | async-done | bytes 1048608 | tf_op jit(solution)/shard_map/all_to_all | solution.py:93
  103.1 1.0 fusion.20
  104.2 1.1 broadcast_in_dim.13
  105.3 6.6 %all-to-all-start.2 = ((bf16[8,64,1024]{2,1,0:T(8,128)(2,1)}), bf16[8,64,1024]{2,1,0:T(8,128)(2,1)S(1)}, u32[]{:S(2)}, u32[]{:S(2)}) async-start(bf16[8,64,1024]{2,1,0:T(8,128)(2,1)} %broadcast_in_dim.13), calls=%async_computation.2 | async-start | bytes 2097152 | tf_op jit(solution)/shard_map/all_to_all | solution.py:48
  111.9 0.7 collective-permute-start.14
  112.5 9.7 %all-to-all-done.2.blocks = bf16[8,64,1024]{2,1,0:T(8,128)(2,1)S(1)} async-done(((bf16[8,64,1024]{2,1,0:T(8,128)(2,1)}), bf16[8,64,1024]{2,1,0:T(8,128)(2,1)S(1)}, u32[]{:S(2)}, u32[]{:S(2)}) %all-to-all-start.2) | async-done | bytes 1048608 | tf_op jit(solution)/shard_map/all_to_all | solution.py:48
  122.5 26.2 %all_to_all.20 = bf16[8,128,1024]{2,1,0:T(8,128)(2,1)S(1)} all-to-all(bf16[8,128,1024]{2,1,0:T(8,128)(2,1)S(1)} %broadcast_in_dim.14), channel_id=1, replica_groups=mesh['x'=4,'yl'=2,'z'=4,'yh'=2,'k'=2] {'z','yh'}, dimensions={0} | all-to-all | bytes 4194304 | tf_op jit(solution)/shard_map/all_to_all | solution.py:48
  148.6 11.1 %collective-permute-start.15 = (bf16[8,128,1024]{2,1,0:T(8,128)(2,1)S(1)}, bf16[8,128,1024]{2,1,0:T(8,128)(2,1)}, u32[]{:S(2)}, u32[]{:S(2)}) collective-permute-start(bf16[8,128,1024]{2,1,0:T(8,128)(2,1)S(1)} %all_to_all.20), channel_id=1, source_target_pairs={{0,1},{1,0},{2,3},{3,2},{4,5},{5,4},{6,7},{7,6},{8,9},{9,8},{10,11... | collective-permute-start | bytes 6291464 | tf_op jit(solution)/shard_map/ppermute | solution.py:30
  159.8 0.6 placed.1
  160.6 0.8 fusion.4
  161.3 0.8 fusion.7
  162.1 2.2 %collective-permute-done.16 = bf16[8,64,512]{2,1,0:T(8,128)(2,1)S(1)} collective-permute-done((bf16[8,64,512]{2,1,0:T(8,128)(2,1)S(1)}, bf16[8,64,512]{2,1,0:T(8,128)(2,1)S(1)}, u32[]{:S(2)}, u32[]{:S(2)}) %collective-permute-start.16) | collective-permute-done | bytes 524320 | tf_op jit(solution)/shard_map/ppermute | solution.py:30
  164.2 3.3 %fusion.1 = f32[1024,512]{1,0:T(8,128)} fusion(f32[1024,512,1]{1,0,2:T(8,128)S(1)} %fusion.4, bf16[8,64,512]{2,1,0:T(8,128)(2,1)S(1)} %collective-permute-done.16, bf16[8,128,1024]{2,1,0:T(8,128)(2,1)} %collective-permute-done.15), kind=kOutput, calls=%fused_computation.5 | convolution fusion | flops 537919488 | bytes 5767168 | tf_op jit(solution)/shard_map/dot_general | solution.py:123
  167.5 3.3 %fusion.2 = f32[1024,512]{1,0:T(8,128)} fusion(f32[1024,512,1]{1,0,2:T(8,128)S(1)} %fusion.7, bf16[8,64,512]{2,1,0:T(8,128)(2,1)S(1)} %collective-permute-done.16, bf16[8,128,1024]{2,1,0:T(8,128)(2,1)} %collective-permute-done.15), kind=kOutput, calls=%fused_computation.7 | convolution fusion | flops 537919488 | bytes 5767168 | tf_op jit(solution)/shard_map/dot_general | solution.py:123
  (58 shorter events, 2.5 us)
Async XLA Ops:
  0.6 15.9 %collective-permute-start = (bf16[64,3584]{1,0:T(8,128)(2,1)}, bf16[64,3584]{1,0:T(8,128)(2,1)S(1)}, u32[]{:S(2)}, u32[]{:S(2)}) collective-permute-start(bf16[64,3584]{1,0:T(8,128)(2,1)} %param.5), channel_id=1, source_target_pairs={{0,2},{2,0},{4,6},{6,4},{8,10},{10,8},{12,14},{14,12},{1,3},{3,1},... | collective-permute-start | bytes 1376264 | tf_op jit(solution)/shard_map/ppermute | solution.py:26
  4.5 13.9 %collective-permute-start.1 = (bf16[64,3584]{1,0:T(8,128)(2,1)}, bf16[64,3584]{1,0:T(8,128)(2,1)S(1)}, u32[]{:S(2)}, u32[]{:S(2)}) collective-permute-start(bf16[64,3584]{1,0:T(8,128)(2,1)} %param.5), channel_id=1, source_target_pairs={{0,4},{2,6},{4,8},{6,10},{8,12},{10,14},{12,0},{14,2},{1,5},{3,7},... | collective-permute-start | bytes 1376264 | tf_op jit(solution)/shard_map/ppermute | solution.py:26
  6.1 12.3 %collective-permute-start.2 = (bf16[64,3584]{1,0:T(8,128)(2,1)}, bf16[64,3584]{1,0:T(8,128)(2,1)S(1)}, u32[]{:S(2)}, u32[]{:S(2)}) collective-permute-start(bf16[64,3584]{1,0:T(8,128)(2,1)} %param.5), channel_id=1, source_target_pairs={{0,12},{2,14},{4,0},{6,2},{8,4},{10,6},{12,8},{14,10},{1,13},{3,15... | collective-permute-start | bytes 1376264 | tf_op jit(solution)/shard_map/ppermute | solution.py:26
  8.2 63.9 %collective-permute-start.12 = (bf16[3584,512]{1,0:T(8,128)(2,1)}, bf16[3584,512]{1,0:T(8,128)(2,1)}, u32[]{:S(2)}, u32[]{:S(2)}) collective-permute-start(bf16[3584,512]{1,0:T(8,128)(2,1)} %param.6), channel_id=1, source_target_pairs={{0,1},{1,0},{2,3},{3,2},{4,5},{5,4},{6,7},{7,6},{8,9},{9,8},{10,11... | collective-permute-start | bytes 11010056 | tf_op jit(solution)/shard_map/ppermute | solution.py:30
  12.4 4.1 %copy-start.3 = (bf16[64,3584]{1,0:T(8,128)(2,1)S(1)}, bf16[64,3584]{1,0:T(8,128)(2,1)}, u32[]{:S(2)}) copy-start(bf16[64,3584]{1,0:T(8,128)(2,1)} %param.4) | copy-start | bytes 1376260
  16.5 7.3 %copy-start.7 = (bf16[256,3584]{1,0:T(8,128)(2,1)S(1)}, bf16[256,3584]{1,0:T(8,128)(2,1)}, u32[]{:S(2)}) copy-start(bf16[256,3584]{1,0:T(8,128)(2,1)} %constant_dynamic-update-slice_fusion.5) | copy-start | bytes 5505028
  18.5 16.7 %collective-permute-start.3 = (bf16[96,3584]{1,0:T(8,128)(2,1)S(1)}, bf16[96,3584]{1,0:T(8,128)(2,1)S(1)}, u32[]{:S(2)}, u32[]{:S(2)}) collective-permute-start(bf16[96,3584]{1,0:T(8,128)(2,1)S(1)} %get-tuple-element.63), channel_id=1, source_target_pairs={{0,4},{2,6},{4,8},{6,10},{8,12},{10,14},{12,0},{14,2},{1,5},{3,7},... | collective-permute-start | bytes 2064392 | tf_op jit(solution)/shard_map/ppermute | solution.py:26
  18.9 16.3 %collective-permute-start.4 = (bf16[96,3584]{1,0:T(8,128)(2,1)S(1)}, bf16[96,3584]{1,0:T(8,128)(2,1)S(1)}, u32[]{:S(2)}, u32[]{:S(2)}) collective-permute-start(bf16[96,3584]{1,0:T(8,128)(2,1)S(1)} %get-tuple-element.62), channel_id=1, source_target_pairs={{0,12},{2,14},{4,0},{6,2},{8,4},{10,6},{12,8},{14,10},{1,13},{3,15... | collective-permute-start | bytes 2064392 | tf_op jit(solution)/shard_map/ppermute | solution.py:26
  21.3 11.4 %collective-permute-start.5 = (bf16[64,3584]{1,0:T(8,128)(2,1)S(1)}, bf16[64,3584]{1,0:T(8,128)(2,1)S(1)}, u32[]{:S(2)}, u32[]{:S(2)}) collective-permute-start(bf16[64,3584]{1,0:T(8,128)(2,1)S(1)} %copy-done.3), channel_id=1, source_target_pairs={{0,2},{2,0},{4,6},{6,4},{8,10},{10,8},{12,14},{14,12},{1,3},{3,1},... | collective-permute-start | bytes 1376264 | tf_op jit(solution)/shard_map/ppermute | solution.py:26
  21.6 26.0 %collective-permute-start.8 = (bf16[3584,512]{1,0:T(8,128)(2,1)S(1)}, bf16[3584,512]{1,0:T(8,128)(2,1)S(1)}, u32[]{:S(2)}, u32[]{:S(2)}) collective-permute-start(bf16[3584,512]{1,0:T(8,128)(2,1)S(1)} %fusion), channel_id=1, source_target_pairs={{0,1},{1,0},{2,3},{3,2},{4,5},{5,4},{6,7},{7,6},{8,9},{9,8},{10,11... | collective-permute-start | bytes 11010056 | tf_op jit(solution)/shard_map/ppermute | solution.py:30
  32.7 3.3 %copy-start.5 = (bf16[64,3584]{1,0:T(8,128)(2,1)}, bf16[64,3584]{1,0:T(8,128)(2,1)S(1)}, u32[]{:S(2)}) copy-start(bf16[64,3584]{1,0:T(8,128)(2,1)S(1)} %collective-permute-done.5) | copy-start | bytes 1376260
  35.4 11.1 %collective-permute-start.9 = (bf16[64,3584]{1,0:T(8,128)(2,1)S(1)}, bf16[64,3584]{1,0:T(8,128)(2,1)S(1)}, u32[]{:S(2)}, u32[]{:S(2)}) collective-permute-start(bf16[64,3584]{1,0:T(8,128)(2,1)S(1)} %pad_maximum_fusion.4), channel_id=1, source_target_pairs={{0,2},{2,0},{4,6},{6,4},{8,10},{10,8},{12,14},{14,12},{1,3},{3,1},... | collective-permute-start | bytes 1376264 | tf_op jit(solution)/shard_map/ppermute | solution.py:26
  36.0 20.7 %collective-permute-start.6 = (bf16[128,3584]{1,0:T(8,128)(2,1)S(1)}, bf16[128,3584]{1,0:T(8,128)(2,1)}, u32[]{:S(2)}, u32[]{:S(2)}) collective-permute-start(bf16[128,3584]{1,0:T(8,128)(2,1)S(1)} %constant_dynamic-update-slice_fusion), channel_id=1, source_target_pairs={{0,4},{2,6},{4,8},{6,10},{8,12},{10,14},{12,0},{14,2},{1,5},{3,7},... | collective-permute-start | bytes 2752520 | tf_op jit(solution)/shard_map/ppermute | solution.py:26
  36.5 20.1 %collective-permute-start.7 = (bf16[128,3584]{1,0:T(8,128)(2,1)S(1)}, bf16[128,3584]{1,0:T(8,128)(2,1)}, u32[]{:S(2)}, u32[]{:S(2)}) collective-permute-start(bf16[128,3584]{1,0:T(8,128)(2,1)S(1)} %constant_dynamic-update-slice_fusion), channel_id=1, source_target_pairs={{0,12},{2,14},{4,0},{6,2},{8,4},{10,6},{12,8},{14,10},{1,13},{3,15... | collective-permute-start | bytes 2752520 | tf_op jit(solution)/shard_map/ppermute | solution.py:26
  56.7 19.5 %all-to-all-start = ((bf16[8,64,1024]{2,1,0:T(8,128)(2,1)}), bf16[8,64,1024]{2,1,0:T(8,128)(2,1)S(1)}, u32[]{:S(2)}, u32[]{:S(2)}) async-start(bf16[8,64,1024]{2,1,0:T(8,128)(2,1)} %fusion.44), calls=%async_computation | async-start | bytes 2097152 | tf_op jit(solution)/shard_map/all_to_all | solution.py:93
  61.1 6.9 %copy-start.4 = (bf16[64,3584]{1,0:T(8,128)(2,1)S(1)}, bf16[64,3584]{1,0:T(8,128)(2,1)}, u32[]{:S(2)}) copy-start(bf16[64,3584]{1,0:T(8,128)(2,1)} %param.4) | copy-start | bytes 1376260
  61.1 6.9 %copy-start.6 = (bf16[64,3584]{1,0:T(8,128)(2,1)S(1)}, bf16[64,3584]{1,0:T(8,128)(2,1)}, u32[]{:S(2)}) copy-start(bf16[64,3584]{1,0:T(8,128)(2,1)} %copy-done.5) | copy-start | bytes 1376260
  63.4 13.2 %collective-permute-start.10 = (bf16[64,3584]{1,0:T(8,128)(2,1)}, bf16[64,3584]{1,0:T(8,128)(2,1)}, u32[]{:S(2)}, u32[]{:S(2)}) collective-permute-start(bf16[64,3584]{1,0:T(8,128)(2,1)} %get-tuple-element.55), channel_id=1, source_target_pairs={{0,4},{2,6},{4,8},{6,10},{8,12},{10,14},{12,0},{14,2},{1,5},{3,7},... | collective-permute-start | bytes 1376264 | tf_op jit(solution)/shard_map/ppermute | solution.py:26
  65.4 11.1 %collective-permute-start.11 = (bf16[64,3584]{1,0:T(8,128)(2,1)}, bf16[64,3584]{1,0:T(8,128)(2,1)}, u32[]{:S(2)}, u32[]{:S(2)}) collective-permute-start(bf16[64,3584]{1,0:T(8,128)(2,1)} %get-tuple-element.57), channel_id=1, source_target_pairs={{0,12},{2,14},{4,0},{6,2},{8,4},{10,6},{12,8},{14,10},{1,13},{3,15... | collective-permute-start | bytes 1376264 | tf_op jit(solution)/shard_map/ppermute | solution.py:26
  76.2 1.0 copy-start.2
  80.8 3.7 %copy-start = (f32[256,512]{1,0:T(8,128)S(1)}, f32[256,512]{1,0:T(8,128)}, u32[]{:S(2)}) copy-start(f32[256,512]{1,0:T(8,128)} %fusion.17) | copy-start | bytes 1572868
  80.8 3.7 %copy-start.1 = (f32[256,512]{1,0:T(8,128)S(1)}, f32[256,512]{1,0:T(8,128)}, u32[]{:S(2)}) copy-start(f32[256,512]{1,0:T(8,128)} %fusion.16) | copy-start | bytes 1572868
  86.7 16.3 %all-to-all-start.1 = ((bf16[8,64,1024]{2,1,0:T(8,128)(2,1)}), bf16[8,64,1024]{2,1,0:T(8,128)(2,1)S(1)}, u32[]{:S(2)}, u32[]{:S(2)}) async-start(bf16[8,64,1024]{2,1,0:T(8,128)(2,1)} %get-tuple-element.44), calls=%async_computation.1 | async-start | bytes 2097152 | tf_op jit(solution)/shard_map/all_to_all | solution.py:93
  91.8 12.4 %collective-permute-start.13 = (bf16[64,1024]{1,0:T(8,128)(2,1)S(1)}, bf16[64,1024]{1,0:T(8,128)(2,1)S(1)}, u32[]{:S(2)}, u32[]{:S(2)}) collective-permute-start(bf16[64,1024]{1,0:T(8,128)(2,1)S(1)} %fusion.18), channel_id=1, source_target_pairs={{0,0},{1,1},{2,16},{3,17},{4,32},{5,33},{6,48},{7,49},{8,64},{9,65... | collective-permute-start | bytes 393224 | tf_op jit(solution)/shard_map/ppermute | solution.py:43
  105.3 16.9 %all-to-all-start.2 = ((bf16[8,64,1024]{2,1,0:T(8,128)(2,1)}), bf16[8,64,1024]{2,1,0:T(8,128)(2,1)S(1)}, u32[]{:S(2)}, u32[]{:S(2)}) async-start(bf16[8,64,1024]{2,1,0:T(8,128)(2,1)} %broadcast_in_dim.13), calls=%async_computation.2 | async-start | bytes 2097152 | tf_op jit(solution)/shard_map/all_to_all | solution.py:48
  111.9 0.7 collective-permute-start.14
  148.6 15.6 %collective-permute-start.15 = (bf16[8,128,1024]{2,1,0:T(8,128)(2,1)S(1)}, bf16[8,128,1024]{2,1,0:T(8,128)(2,1)}, u32[]{:S(2)}, u32[]{:S(2)}) collective-permute-start(bf16[8,128,1024]{2,1,0:T(8,128)(2,1)S(1)} %all_to_all.20), channel_id=1, source_target_pairs={{0,1},{1,0},{2,3},{3,2},{4,5},{5,4},{6,7},{7,6},{8,9},{9,8},{10,11... | collective-permute-start | bytes 6291464 | tf_op jit(solution)/shard_map/ppermute | solution.py:30
  160.5 3.8 %collective-permute-start.16 = (bf16[8,64,512]{2,1,0:T(8,128)(2,1)S(1)}, bf16[8,64,512]{2,1,0:T(8,128)(2,1)S(1)}, u32[]{:S(2)}, u32[]{:S(2)}) collective-permute-start(bf16[8,64,512]{2,1,0:T(8,128)(2,1)S(1)} %constant_dynamic-slice_fusion), channel_id=1, source_target_pairs={{0,1},{1,0},{2,3},{3,2},{4,5},{5,4},{6,7},{7,6},{8,9},{9,8},{10,11... | collective-permute-start | bytes 1572872 | tf_op jit(solution)/shard_map/ppermute | solution.py:30

commit v3 on v2

--- a/solution.py
+++ b/solution.py
@@ -71,21 +71,36 @@
     return jnp.concatenate([jnp.concatenate(h, 2) for h in (first, second)], 0)
 
 
-def place_kernel(at_ref, blocks, out):
-    for i in range(8):
-        out[at_ref[i]] = blocks[i]
+def arrange_kernel(at_ref, pair, up, down, across, side_across, out):
+    n = across.shape[0]
+    blocks = [pair[:n], pair[n:], up[:n], down[:n], up[n:], down[n:], across[...], side_across[...]]
+    for i, b in enumerate(blocks):
+        out[at_ref[i]] = b
 
 
-def placed(blocks, at):
+def arranged(parts, at):
     vmem = pl.BlockSpec(memory_space=pltpu.VMEM)
     return pl.pallas_call(
-        place_kernel,
-        in_specs=[pl.BlockSpec(memory_space=pltpu.SMEM), vmem],
+        arrange_kernel,
+        in_specs=[pl.BlockSpec(memory_space=pltpu.SMEM)] + [vmem] * 5,
         out_specs=vmem,
-        out_shape=jax.ShapeDtypeStruct(blocks.shape, BF),
+        out_shape=jax.ShapeDtypeStruct((8,) + parts[3].shape, BF),
         compiler_params=pltpu.CompilerParams(vmem_limit_bytes=4 * 1024 * 1024),
-        name="placed",
-    )(jnp.stack(at).astype(jnp.int32), blocks)
+        name="arranged",
+    )(jnp.stack(at).astype(jnp.int32), *parts)
+
+
+def start_around(a, axes):
+    return jnp.concatenate([a, step(a, 0, 1, axes)], 0)
+
+
+def ends_around(pair, axes):
+    return step(pair, 1, 0, axes), step(pair, 3, 0, axes)
+
+
+def finish_around(pair, up, down, axes):
+    n = pair.shape[0] // 2
+    return pair, up, down, step(up[:n], 1, 0, axes), step(down[n:], 3, 0, axes)
 
 
 def summed(sent, partial):
@@ -104,13 +119,15 @@
     return out
 
 
-def columns(blocks):
+def columns(parts):
     x, yl, z, yh = (lax.axis_index(a) for a in ROW + SIDE)
     number = [PLACES.index((i // 2, i % 2)) for i in range(8)]
     at = []
     for a, b in PLACES:
-        at.append(lookup(number, (z - x + a + 4) % 4 * 2 + (yh - yl + b + 2) % 2))
-    every = placed(blocks, at)
+        member = (x + a) % 4 * 2 + (yl + b) % 2
+        far = [lookup([place[q] for place in PLACES], member) for q in range(2)]
+        at.append(lookup(number, (z - x + far[0] + 4) % 4 * 2 + (yh - yl + far[1] + 2) % 2))
+    every = arranged(parts, at)
     k = lax.axis_index("k")
     half = every.shape[2] // 2
     mine = lax.dynamic_slice_in_dim(every, k * half, half, 2)
@@ -158,10 +175,12 @@
     t_p = transposed(p)
     d, p, t_p = lax.optimization_barrier((d, p, t_p))
     t_d = transposed(d)
-    every = spread(p, ROW)
-    t_d, every = lax.optimization_barrier((t_d, every))
+    cols_pair = start_around(p, ROW)
+    t_d, cols_pair = lax.optimization_barrier((t_d, cols_pair))
     rows = spread(jnp.concatenate([t_p, t_d], 0), SIDE)
-    cols = columns(every)
+    cols_ends = ends_around(cols_pair, ROW)
+    cols = columns(finish_around(cols_pair, *cols_ends, ROW))
+    rows, *cols = lax.optimization_barrier((rows, *cols))
     others = swap(rows)
     gram_tile = (product(rows[:, :n], cols[0]) + product(others[:, :n], cols[1])) / tokens
     cross_tile = (product(rows[:, n:], cols[0]) + product(others[:, n:], cols[1])) / tokens

time: 172 us -> 167 us (0.971)
  blocking collectives: 26.2 us -> 0 us
  starting transfers between devices: 48.6 us -> 68.9 us
    all_to_all x1 -> x0, blocking collectives: 26.2 us -> none  [spread(): lax.all_to_all(jnp.broadcast_to(a, (n,) + a.shape), axes, 0, 0, tiled=True)]
    all_to_all x1, waiting for transfers between devices: 9.66 us -> 0.01 us  [spread(): lax.all_to_all(jnp.broadcast_to(a, (n,) + a.shape), axes, 0, 0, tiled=True)]
    ppermute x11 -> x16, waiting for transfers between devices: 25.3 us -> 34.8 us  [step(): return lax.ppermute(a, axes, pairs)]
    all_to_all x1, starting transfers between devices: 6.58 us -> 16 us  [spread(): lax.all_to_all(jnp.broadcast_to(a, (n,) + a.shape), axes, 0, 0, tiled=True)]
    ppermute x11 -> x16, starting transfers between devices: 16.6 us -> 23.2 us  [step(): return lax.ppermute(a, axes, pairs)]
    ppermute x4, starting transfers between devices: 14.5 us -> 18.9 us  [swap(): return lax.ppermute(a, 'k', [(0, 1), (1, 0)])]
    ppermute x4, waiting for transfers between devices: 2.18 us -> 3.95 us  [swap(): return lax.ppermute(a, 'k', [(0, 1), (1, 0)])]
  transfers between devices with their start and end apart: 20 -> 25, of which waited for: 8 -> 11; matrix products, arithmetic and copies ran while one was open for 17% -> 17% of each run, Pallas kernels for 0% -> 0%
where the time goes in v3:
time: 167 us
  starting transfers between devices  68.9 us (41%)
  waiting for transfers between devices  49.3 us (30%)
  matrix products  31.6 us (19%)
  local copies, waits for them, and re-layouts  8.95 us (5%)
  other arithmetic  6.19 us (4%)
    ppermute x16, waiting for transfers between devices, step(): return lax.ppermute(a, axes, pairs)  34.8 us
    ppermute x16, starting transfers between devices, step(): return lax.ppermute(a, axes, pairs)  23.2 us
    dot_general x8, matrix products, dots(): outs = [jnp.dot(a, w, preferred_element_type=F32) for w in weights]  19.8 us
    ppermute x4, starting transfers between devices, swap(): return lax.ppermute(a, 'k', [(0, 1), (1, 0)])  18.9 us
    all_to_all x1, starting transfers between devices, spread(): lax.all_to_all(jnp.broadcast_to(a, (n,) + a.shape), axes, 0, 0, tiled=True)  16 us
    all_to_all x2, waiting for transfers between devices, summed(): came = lax.all_to_all(sent, ROW, 0, 0, tiled=True)  10.5 us
    all_to_all x2, starting transfers between devices, summed(): came = lax.all_to_all(sent, ROW, 0, 0, tiled=True)  9.54 us
    dot_general x4, matrix products, product(): return lax.dot_general(rows, cols, dims, preferred_element_type=F32)  7.74 us
  transfers between devices with their start and end apart: 25, of which 11 were waited for; matrix products, arithmetic and copies ran while one was open for 17% of the time, Pallas kernels for 0%

profile of v3, /device:TPU:1, one launch (start us, length us, event | category | flops | bytes accessed | tf_op | source)
XLA Modules:
  0.0 166.6 jit_solution(35654366721268208)
XLA Ops:
  0.6 3.8 %collective-permute-start = (bf16[64,3584]{1,0:T(8,128)(2,1)}, bf16[64,3584]{1,0:T(8,128)(2,1)S(1)}, u32[]{:S(2)}, u32[]{:S(2)}) collective-permute-start(bf16[64,3584]{1,0:T(8,128)(2,1)} %param.5), channel_id=1, source_target_pairs={{0,2},{2,0},{4,6},{6,4},{8,10},{10,8},{12,14},{14,12},{1,3},{3,1},... | collective-permute-start | bytes 1376264 | tf_op jit(solution)/shard_map/ppermute | solution.py:26
  4.5 1.6 collective-permute-start.1
  6.1 2.1 %collective-permute-start.2 = (bf16[64,3584]{1,0:T(8,128)(2,1)}, bf16[64,3584]{1,0:T(8,128)(2,1)S(1)}, u32[]{:S(2)}, u32[]{:S(2)}) collective-permute-start(bf16[64,3584]{1,0:T(8,128)(2,1)} %param.5), channel_id=1, source_target_pairs={{0,12},{2,14},{4,0},{6,2},{8,4},{10,6},{12,8},{14,10},{1,13},{3,15... | collective-permute-start | bytes 1376264 | tf_op jit(solution)/shard_map/ppermute | solution.py:26
  8.2 1.2 collective-permute-start.12
  9.5 1.8 %constant_dynamic-update-slice_fusion.5 = bf16[256,3584]{1,0:T(8,128)(2,1)} fusion(bf16[64,3584]{1,0:T(8,128)(2,1)} %param.5), kind=kLoop, calls=%fused_computation.51 | loop fusion | bytes 917504
  11.3 1.1 and_convert_fusion
  12.4 4.1 %fusion = bf16[3584,512]{1,0:T(8,128)(2,1)S(1)} fusion(bf16[3584,512]{1,0:T(8,128)(2,1)} %param.6, s32[512]{0:T(512)S(1)} %get-tuple-element.78, bf16[32,3584]{1,0:T(8,128)(2,1)S(1)} %get-tuple-element.73, bf16[32,3584]{1,0:T(8,128)(2,1)S(1)} %get-tuple-element.72, s32[512]{0:T(512)S(1)} %get-tuple-element.79), kind=kOutput, calls=%fused_computation.1 | convolution fusion | flops 245006336 | bytes 7802880 | tf_op jit(solution)/shard_map/dot_general | solution.py:59
  16.5 1.8 %collective-permute-done.1 = bf16[64,3584]{1,0:T(8,128)(2,1)S(1)} collective-permute-done((bf16[64,3584]{1,0:T(8,128)(2,1)}, bf16[64,3584]{1,0:T(8,128)(2,1)S(1)}, u32[]{:S(2)}, u32[]{:S(2)}) %collective-permute-start.1) | collective-permute-done | bytes 458784 | tf_op jit(solution)/shard_map/ppermute | solution.py:26
  18.9 2.3 %collective-permute-start.4 = (bf16[96,3584]{1,0:T(8,128)(2,1)S(1)}, bf16[96,3584]{1,0:T(8,128)(2,1)S(1)}, u32[]{:S(2)}, u32[]{:S(2)}) collective-permute-start(bf16[96,3584]{1,0:T(8,128)(2,1)S(1)} %get-tuple-element.70), channel_id=1, source_target_pairs={{0,12},{2,14},{4,0},{6,2},{8,4},{10,6},{12,8},{14,10},{1,13},{3,15... | collective-permute-start | bytes 2064392 | tf_op jit(solution)/shard_map/ppermute | solution.py:26
  21.6 2.1 %collective-permute-start.8 = (bf16[3584,512]{1,0:T(8,128)(2,1)S(1)}, bf16[3584,512]{1,0:T(8,128)(2,1)S(1)}, u32[]{:S(2)}, u32[]{:S(2)}) collective-permute-start(bf16[3584,512]{1,0:T(8,128)(2,1)S(1)} %fusion), channel_id=1, source_target_pairs={{0,1},{1,0},{2,3},{3,2},{4,5},{5,4},{6,7},{7,6},{8,9},{9,8},{10,11... | collective-permute-start | bytes 11010056 | tf_op jit(solution)/shard_map/ppermute | solution.py:30
  23.8 1.1 fusion.48
  25.0 7.7 %collective-permute-done.5 = bf16[64,3584]{1,0:T(8,128)(2,1)S(1)} collective-permute-done((bf16[64,3584]{1,0:T(8,128)(2,1)S(1)}, bf16[64,3584]{1,0:T(8,128)(2,1)S(1)}, u32[]{:S(2)}, u32[]{:S(2)}) %collective-permute-start.5) | collective-permute-done | bytes 458784 | tf_op jit(solution)/shard_map/ppermute | solution.py:26
  32.7 2.5 %collective-permute-done.3 = bf16[96,3584]{1,0:T(8,128)(2,1)S(1)} collective-permute-done((bf16[96,3584]{1,0:T(8,128)(2,1)S(1)}, bf16[96,3584]{1,0:T(8,128)(2,1)S(1)}, u32[]{:S(2)}, u32[]{:S(2)}) %collective-permute-start.3) | collective-permute-done | bytes 688160 | tf_op jit(solution)/shard_map/ppermute | solution.py:26
  36.5 2.2 %collective-permute-start.7 = (bf16[128,3584]{1,0:T(8,128)(2,1)S(1)}, bf16[128,3584]{1,0:T(8,128)(2,1)}, u32[]{:S(2)}, u32[]{:S(2)}) collective-permute-start(bf16[128,3584]{1,0:T(8,128)(2,1)S(1)} %constant_dynamic-update-slice_fusion), channel_id=1, source_target_pairs={{0,12},{2,14},{4,0},{6,2},{8,4},{10,6},{12,8},{14,10},{1,13},{3,15... | collective-permute-start | bytes 2752520 | tf_op jit(solution)/shard_map/ppermute | solution.py:26
  38.7 7.8 %collective-permute-done.9 = bf16[64,3584]{1,0:T(8,128)(2,1)S(1)} collective-permute-done((bf16[64,3584]{1,0:T(8,128)(2,1)S(1)}, bf16[64,3584]{1,0:T(8,128)(2,1)S(1)}, u32[]{:S(2)}, u32[]{:S(2)}) %collective-permute-start.9) | collective-permute-done | bytes 458784 | tf_op jit(solution)/shard_map/ppermute | solution.py:26
  46.6 1.1 fusion.50
  47.7 1.1 fusion.51
  48.8 1.1 fusion.49
  49.9 1.1 fusion.40
  51.2 5.5 %collective-permute-done.6 = bf16[128,3584]{1,0:T(8,128)(2,1)} collective-permute-done((bf16[128,3584]{1,0:T(8,128)(2,1)S(1)}, bf16[128,3584]{1,0:T(8,128)(2,1)}, u32[]{:S(2)}, u32[]{:S(2)}) %collective-permute-start.6) | collective-permute-done | bytes 917536 | tf_op jit(solution)/shard_map/ppermute | solution.py:26
  56.7 4.4 %all-to-all-start = ((bf16[8,64,1024]{2,1,0:T(8,128)(2,1)}), bf16[8,64,1024]{2,1,0:T(8,128)(2,1)S(1)}, u32[]{:S(2)}, u32[]{:S(2)}) async-start(bf16[8,64,1024]{2,1,0:T(8,128)(2,1)} %fusion.40), calls=%async_computation | async-start | bytes 2097152 | tf_op jit(solution)/shard_map/all_to_all | solution.py:108
  61.1 2.2 %fusion.42 = (bf16[64,3584]{1,0:T(8,128)(2,1)}, bf16[64,3584]{1,0:T(8,128)(2,1)}) fusion(bf16[128,3584]{1,0:T(8,128)(2,1)} %collective-permute-done.6), kind=kLoop, calls=%fused_computation.89 | loop fusion | bytes 1835008 | tf_op jit(solution)/shard_map/slice | solution.py:170
  63.4 2.0 %fusion.43 = (bf16[64,3584]{1,0:T(8,128)(2,1)S(1)}, bf16[64,3584]{1,0:T(8,128)(2,1)}) fusion(bf16[128,3584]{1,0:T(8,128)(2,1)} %collective-permute-done.7), kind=kLoop, calls=%fused_computation.90 | loop fusion | bytes 1835008 | tf_op jit(solution)/shard_map/slice | solution.py:168
  65.4 2.6 %collective-permute-start.11 = (bf16[64,3584]{1,0:T(8,128)(2,1)}, bf16[64,3584]{1,0:T(8,128)(2,1)}, u32[]{:S(2)}, u32[]{:S(2)}) collective-permute-start(bf16[64,3584]{1,0:T(8,128)(2,1)} %get-tuple-element.65), channel_id=1, source_target_pairs={{0,12},{2,14},{4,0},{6,2},{8,4},{10,6},{12,8},{14,10},{1,13},{3,15... | collective-permute-start | bytes 1376264 | tf_op jit(solution)/shard_map/ppermute | solution.py:26
  68.0 4.1 %fusion.15 = f32[256,512]{1,0:T(8,128)} fusion(bf16[3584,512]{1,0:T(8,128)(2,1)} %param.6, bf16[64,3584]{1,0:T(8,128)(2,1)S(1)} %get-tuple-element.64, bf16[64,3584]{1,0:T(8,128)(2,1)} %get-tuple-element.63, bf16[64,3584]{1,0:T(8,128)(2,1)S(1)} %copy-done.6, bf16[64,3584]{1,0:T(8,128)(2,1)S(1)} %copy-done.4), kind=kOutput, calls=%fused_computation.31 | convolution fusion | flops 946864128 | bytes 6029312 | tf_op jit(solution)/shard_map/dot_general | solution.py:66
  72.1 4.1 %fusion.14 = f32[256,512]{1,0:T(8,128)} fusion(bf16[3584,512]{1,0:T(8,128)(2,1)} %collective-permute-done.12, bf16[64,3584]{1,0:T(8,128)(2,1)S(1)} %get-tuple-element.64, bf16[64,3584]{1,0:T(8,128)(2,1)} %get-tuple-element.63, bf16[64,3584]{1,0:T(8,128)(2,1)S(1)} %copy-done.6, bf16[64,3584]{1,0:T(8,128)(2,1)S(1)} %copy-done.4), kind=kOutput, calls=%fused_computation.30 | convolution fusion | flops 946864128 | bytes 6029312 | tf_op jit(solution)/shard_map/dot_general | solution.py:66
  77.2 3.6 %fusion.13 = f32[256,512]{1,0:T(8,128)S(1)} fusion(bf16[3584,512]{1,0:T(8,128)(2,1)} %param.6, bf16[64,3584]{1,0:T(8,128)(2,1)} %collective-permute-done.11, bf16[64,3584]{1,0:T(8,128)(2,1)} %collective-permute-done.10, bf16[64,3584]{1,0:T(8,128)(2,1)} %get-tuple-element.65, bf16[64,3584]{1,0:T(8,128)(2,1)S(1)} %copy-done.2), kind=kOutput, calls=%fused_computation.29 | convolution fusion | flops 946864128 | bytes 6029312 | tf_op jit(solution)/shard_map/dot_general | solution.py:66
  80.8 3.6 %fusion.12 = f32[256,512]{1,0:T(8,128)S(1)} fusion(bf16[3584,512]{1,0:T(8,128)(2,1)} %collective-permute-done.12, bf16[64,3584]{1,0:T(8,128)(2,1)} %collective-permute-done.11, bf16[64,3584]{1,0:T(8,128)(2,1)} %collective-permute-done.10, bf16[64,3584]{1,0:T(8,128)(2,1)} %get-tuple-element.65, bf16[64,3584]{1,0:T(8,128)(2,1)S(1)} %copy-done.2), kind=kOutput, calls=%fused_computation.28 | convolution fusion | flops 946864128 | bytes 6029312 | tf_op jit(solution)/shard_map/dot_general | solution.py:66
  84.5 2.2 %fusion.41 = (bf16[8,64,1024]{2,1,0:T(8,128)(2,1)}, f32[8,64,1024]{2,1,0:T(8,128)}) fusion(f32[8,64,1024]{2,1,0:T(8,128)S(1)} %maximum_maximum_fusion, f32[4,64,512]{2,1,0:T(8,128)S(1)} %bitcast.69, f32[4,64,512]{2,1,0:T(8,128)S(1)} %bitcast.68, f32[4,64,512]{2,1,0:T(8,128)S(1)} %bitcast.67, f32[4,64,512]{2,1,0:T(8,128)S(1)} %bitcast.66), kind=kLoop, calls=%fused_computation.88 | loop fusion | flops 2621440 | bytes 7340032 | tf_op jit(solution)/shard_map/convert_element_type | solution.py:172
  86.7 5.1 %all-to-all-start.1 = ((bf16[8,64,1024]{2,1,0:T(8,128)(2,1)}), bf16[8,64,1024]{2,1,0:T(8,128)(2,1)S(1)}, u32[]{:S(2)}, u32[]{:S(2)}) async-start(bf16[8,64,1024]{2,1,0:T(8,128)(2,1)} %get-tuple-element.47), calls=%async_computation.1 | async-start | bytes 2097152 | tf_op jit(solution)/shard_map/all_to_all | solution.py:108
  92.5 10.5 %all-to-all-done.1 = bf16[8,64,1024]{2,1,0:T(8,128)(2,1)S(1)} async-done(((bf16[8,64,1024]{2,1,0:T(8,128)(2,1)}), bf16[8,64,1024]{2,1,0:T(8,128)(2,1)S(1)}, u32[]{:S(2)}, u32[]{:S(2)}) %all-to-all-start.1) | async-done | bytes 1048608 | tf_op jit(solution)/shard_map/all_to_all | solution.py:108
  103.1 1.0 fusion.18
  104.2 1.1 collective-permute-start.15
  106.0 3.6 %collective-permute-done.15 = bf16[64,1024]{1,0:T(8,128)(2,1)S(1)} collective-permute-done((bf16[64,1024]{1,0:T(8,128)(2,1)S(1)}, bf16[64,1024]{1,0:T(8,128)(2,1)S(1)}, u32[]{:S(2)}, u32[]{:S(2)}) %collective-permute-start.15) | collective-permute-done | bytes 131104 | tf_op jit(solution)/shard_map/ppermute | solution.py:26
  109.6 1.6 broadcast_in_dim.10
  111.2 16.0 %all-to-all-start.2 = ((bf16[8,128,1024]{2,1,0:T(8,128)(2,1)}), bf16[8,128,1024]{2,1,0:T(8,128)(2,1)S(1)}, u32[]{:S(2)}, u32[]{:S(2)}) async-start(bf16[8,128,1024]{2,1,0:T(8,128)(2,1)} %broadcast_in_dim.10), calls=%async_computation.2 | async-start | bytes 4194304 | tf_op jit(solution)/shard_map/all_to_all | solution.py:48
  127.1 2.7 %collective-permute-start.17 = (bf16[128,1024]{1,0:T(8,128)(2,1)S(1)}, bf16[128,1024]{1,0:T(8,128)(2,1)S(1)}, u32[]{:S(2)}, u32[]{:S(2)}) collective-permute-start(bf16[128,1024]{1,0:T(8,128)(2,1)S(1)} %pad_maximum_fusion.9.pair), channel_id=1, source_target_pairs={{0,96},{16,112},{32,0},{48,16},{64,32},{80,48},{96,64},{112,80},{1... | collective-permute-start | bytes 786440 | tf_op jit(solution)/shard_map/ppermute | solution.py:26
  129.8 3.8 %collective-permute-done.16.up = bf16[128,1024]{1,0:T(8,128)(2,1)S(1)} collective-permute-done((bf16[128,1024]{1,0:T(8,128)(2,1)S(1)}, bf16[128,1024]{1,0:T(8,128)(2,1)S(1)}, u32[]{:S(2)}, u32[]{:S(2)}) %collective-permute-start.16) | collective-permute-done | bytes 262176 | tf_op jit(solution)/shard_map/ppermute | solution.py:26
  133.7 2.7 %collective-permute-start.19 = (bf16[64,1024]{1,0:T(8,128)(2,1)S(1)}, bf16[64,1024]{1,0:T(8,128)(2,1)S(1)}, u32[]{:S(2)}, u32[]{:S(2)}) collective-permute-start(bf16[64,1024]{1,0:T(8,128)(2,1)S(1)} %slice.87), channel_id=1, source_target_pairs={{0,96},{16,112},{32,0},{48,16},{64,32},{80,48},{96,64},{112,80},{1... | collective-permute-start | bytes 393224 | tf_op jit(solution)/shard_map/ppermute | solution.py:26
  136.5 2.2 %collective-permute-done.18.across = bf16[64,1024]{1,0:T(8,128)(2,1)S(1)} collective-permute-done((bf16[64,1024]{1,0:T(8,128)(2,1)S(1)}, bf16[64,1024]{1,0:T(8,128)(2,1)S(1)}, u32[]{:S(2)}, u32[]{:S(2)}) %collective-permute-start.18) | collective-permute-done | bytes 131104 | tf_op jit(solution)/shard_map/ppermute | solution.py:26
  139.4 10.0 %collective-permute-start.20 = (bf16[8,64,512]{2,1,0:T(8,128)(2,1)S(1)}, bf16[8,64,512]{2,1,0:T(8,128)(2,1)}, u32[]{:S(2)}, u32[]{:S(2)}) collective-permute-start(bf16[8,64,512]{2,1,0:T(8,128)(2,1)S(1)} %get-tuple-element.60), channel_id=1, source_target_pairs={{0,1},{1,0},{2,3},{3,2},{4,5},{5,4},{6,7},{7,6},{8,9},{9,8},{10,11... | collective-permute-start | bytes 1572872 | tf_op jit(solution)/shard_map/ppermute | solution.py:30
  149.4 1.7 %collective-permute-done.20 = bf16[8,64,512]{2,1,0:T(8,128)(2,1)} collective-permute-done((bf16[8,64,512]{2,1,0:T(8,128)(2,1)S(1)}, bf16[8,64,512]{2,1,0:T(8,128)(2,1)}, u32[]{:S(2)}, u32[]{:S(2)}) %collective-permute-start.20) | collective-permute-done | bytes 524320 | tf_op jit(solution)/shard_map/ppermute | solution.py:30
  151.1 5.5 %collective-permute-start.21 = (bf16[8,128,1024]{2,1,0:T(8,128)(2,1)S(1)}, bf16[8,128,1024]{2,1,0:T(8,128)(2,1)S(1)}, u32[]{:S(2)}, u32[]{:S(2)}) collective-permute-start(bf16[8,128,1024]{2,1,0:T(8,128)(2,1)S(1)} %all-to-all-done.2), channel_id=1, source_target_pairs={{0,1},{1,0},{2,3},{3,2},{4,5},{5,4},{6,7},{7,6},{8,9},{9,8},{10,11... | collective-permute-start | bytes 6291464 | tf_op jit(solution)/shard_map/ppermute | solution.py:30
  156.6 0.8 fusion.5
  157.4 0.8 fusion.7
  158.1 2.3 %collective-permute-done.21 = bf16[8,128,1024]{2,1,0:T(8,128)(2,1)S(1)} collective-permute-done((bf16[8,128,1024]{2,1,0:T(8,128)(2,1)S(1)}, bf16[8,128,1024]{2,1,0:T(8,128)(2,1)S(1)}, u32[]{:S(2)}, u32[]{:S(2)}) %collective-permute-start.21) | collective-permute-done | bytes 2097184 | tf_op jit(solution)/shard_map/ppermute | solution.py:30
  160.4 3.1 %fusion.1 = f32[1024,512]{1,0:T(8,128)} fusion(f32[1024,512,1]{1,0,2:T(8,128)S(1)} %fusion.5, bf16[8,64,512]{2,1,0:T(8,128)(2,1)} %collective-permute-done.20, bf16[8,128,1024]{2,1,0:T(8,128)(2,1)S(1)} %collective-permute-done.21), kind=kOutput, calls=%fused_computation.5 | convolution fusion | flops 537919488 | bytes 5767168 | tf_op jit(solution)/shard_map/dot_general | solution.py:140
  163.5 3.1 %fusion.2 = f32[1024,512]{1,0:T(8,128)} fusion(f32[1024,512,1]{1,0,2:T(8,128)S(1)} %fusion.7, bf16[8,64,512]{2,1,0:T(8,128)(2,1)} %collective-permute-done.20, bf16[8,128,1024]{2,1,0:T(8,128)(2,1)S(1)} %collective-permute-done.21), kind=kOutput, calls=%fused_computation.7 | convolution fusion | flops 537919488 | bytes 5767168 | tf_op jit(solution)/shard_map/dot_general | solution.py:140
  (69 shorter events, 6.1 us)
Async XLA Ops:
  0.6 15.9 %collective-permute-start = (bf16[64,3584]{1,0:T(8,128)(2,1)}, bf16[64,3584]{1,0:T(8,128)(2,1)S(1)}, u32[]{:S(2)}, u32[]{:S(2)}) collective-permute-start(bf16[64,3584]{1,0:T(8,128)(2,1)} %param.5), channel_id=1, source_target_pairs={{0,2},{2,0},{4,6},{6,4},{8,10},{10,8},{12,14},{14,12},{1,3},{3,1},... | collective-permute-start | bytes 1376264 | tf_op jit(solution)/shard_map/ppermute | solution.py:26
  4.5 13.9 %collective-permute-start.1 = (bf16[64,3584]{1,0:T(8,128)(2,1)}, bf16[64,3584]{1,0:T(8,128)(2,1)S(1)}, u32[]{:S(2)}, u32[]{:S(2)}) collective-permute-start(bf16[64,3584]{1,0:T(8,128)(2,1)} %param.5), channel_id=1, source_target_pairs={{0,4},{2,6},{4,8},{6,10},{8,12},{10,14},{12,0},{14,2},{1,5},{3,7},... | collective-permute-start | bytes 1376264 | tf_op jit(solution)/shard_map/ppermute | solution.py:26
  6.1 12.3 %collective-permute-start.2 = (bf16[64,3584]{1,0:T(8,128)(2,1)}, bf16[64,3584]{1,0:T(8,128)(2,1)S(1)}, u32[]{:S(2)}, u32[]{:S(2)}) collective-permute-start(bf16[64,3584]{1,0:T(8,128)(2,1)} %param.5), channel_id=1, source_target_pairs={{0,12},{2,14},{4,0},{6,2},{8,4},{10,6},{12,8},{14,10},{1,13},{3,15... | collective-permute-start | bytes 1376264 | tf_op jit(solution)/shard_map/ppermute | solution.py:26
  8.2 63.9 %collective-permute-start.12 = (bf16[3584,512]{1,0:T(8,128)(2,1)}, bf16[3584,512]{1,0:T(8,128)(2,1)}, u32[]{:S(2)}, u32[]{:S(2)}) collective-permute-start(bf16[3584,512]{1,0:T(8,128)(2,1)} %param.6), channel_id=1, source_target_pairs={{0,1},{1,0},{2,3},{3,2},{4,5},{5,4},{6,7},{7,6},{8,9},{9,8},{10,11... | collective-permute-start | bytes 11010056 | tf_op jit(solution)/shard_map/ppermute | solution.py:30
  12.4 4.1 %copy-start.3 = (bf16[64,3584]{1,0:T(8,128)(2,1)S(1)}, bf16[64,3584]{1,0:T(8,128)(2,1)}, u32[]{:S(2)}) copy-start(bf16[64,3584]{1,0:T(8,128)(2,1)} %param.4) | copy-start | bytes 1376260
  16.5 7.3 %copy-start.7 = (bf16[256,3584]{1,0:T(8,128)(2,1)S(1)}, bf16[256,3584]{1,0:T(8,128)(2,1)}, u32[]{:S(2)}) copy-start(bf16[256,3584]{1,0:T(8,128)(2,1)} %constant_dynamic-update-slice_fusion.5) | copy-start | bytes 5505028
  18.5 16.7 %collective-permute-start.3 = (bf16[96,3584]{1,0:T(8,128)(2,1)S(1)}, bf16[96,3584]{1,0:T(8,128)(2,1)S(1)}, u32[]{:S(2)}, u32[]{:S(2)}) collective-permute-start(bf16[96,3584]{1,0:T(8,128)(2,1)S(1)} %get-tuple-element.71), channel_id=1, source_target_pairs={{0,4},{2,6},{4,8},{6,10},{8,12},{10,14},{12,0},{14,2},{1,5},{3,7},... | collective-permute-start | bytes 2064392 | tf_op jit(solution)/shard_map/ppermute | solution.py:26
  18.9 16.3 %collective-permute-start.4 = (bf16[96,3584]{1,0:T(8,128)(2,1)S(1)}, bf16[96,3584]{1,0:T(8,128)(2,1)S(1)}, u32[]{:S(2)}, u32[]{:S(2)}) collective-permute-start(bf16[96,3584]{1,0:T(8,128)(2,1)S(1)} %get-tuple-element.70), channel_id=1, source_target_pairs={{0,12},{2,14},{4,0},{6,2},{8,4},{10,6},{12,8},{14,10},{1,13},{3,15... | collective-permute-start | bytes 2064392 | tf_op jit(solution)/shard_map/ppermute | solution.py:26
  21.3 11.4 %collective-permute-start.5 = (bf16[64,3584]{1,0:T(8,128)(2,1)S(1)}, bf16[64,3584]{1,0:T(8,128)(2,1)S(1)}, u32[]{:S(2)}, u32[]{:S(2)}) collective-permute-start(bf16[64,3584]{1,0:T(8,128)(2,1)S(1)} %copy-done.3), channel_id=1, source_target_pairs={{0,2},{2,0},{4,6},{6,4},{8,10},{10,8},{12,14},{14,12},{1,3},{3,1},... | collective-permute-start | bytes 1376264 | tf_op jit(solution)/shard_map/ppermute | solution.py:26
  21.6 26.0 %collective-permute-start.8 = (bf16[3584,512]{1,0:T(8,128)(2,1)S(1)}, bf16[3584,512]{1,0:T(8,128)(2,1)S(1)}, u32[]{:S(2)}, u32[]{:S(2)}) collective-permute-start(bf16[3584,512]{1,0:T(8,128)(2,1)S(1)} %fusion), channel_id=1, source_target_pairs={{0,1},{1,0},{2,3},{3,2},{4,5},{5,4},{6,7},{7,6},{8,9},{9,8},{10,11... | collective-permute-start | bytes 11010056 | tf_op jit(solution)/shard_map/ppermute | solution.py:30
  32.7 3.3 %copy-start.5 = (bf16[64,3584]{1,0:T(8,128)(2,1)}, bf16[64,3584]{1,0:T(8,128)(2,1)S(1)}, u32[]{:S(2)}) copy-start(bf16[64,3584]{1,0:T(8,128)(2,1)S(1)} %collective-permute-done.5) | copy-start | bytes 1376260
  35.4 11.1 %collective-permute-start.9 = (bf16[64,3584]{1,0:T(8,128)(2,1)S(1)}, bf16[64,3584]{1,0:T(8,128)(2,1)S(1)}, u32[]{:S(2)}, u32[]{:S(2)}) collective-permute-start(bf16[64,3584]{1,0:T(8,128)(2,1)S(1)} %pad_maximum_fusion.4), channel_id=1, source_target_pairs={{0,2},{2,0},{4,6},{6,4},{8,10},{10,8},{12,14},{14,12},{1,3},{3,1},... | collective-permute-start | bytes 1376264 | tf_op jit(solution)/shard_map/ppermute | solution.py:26
  36.0 20.7 %collective-permute-start.6 = (bf16[128,3584]{1,0:T(8,128)(2,1)S(1)}, bf16[128,3584]{1,0:T(8,128)(2,1)}, u32[]{:S(2)}, u32[]{:S(2)}) collective-permute-start(bf16[128,3584]{1,0:T(8,128)(2,1)S(1)} %constant_dynamic-update-slice_fusion), channel_id=1, source_target_pairs={{0,4},{2,6},{4,8},{6,10},{8,12},{10,14},{12,0},{14,2},{1,5},{3,7},... | collective-permute-start | bytes 2752520 | tf_op jit(solution)/shard_map/ppermute | solution.py:26
  36.5 20.1 %collective-permute-start.7 = (bf16[128,3584]{1,0:T(8,128)(2,1)S(1)}, bf16[128,3584]{1,0:T(8,128)(2,1)}, u32[]{:S(2)}, u32[]{:S(2)}) collective-permute-start(bf16[128,3584]{1,0:T(8,128)(2,1)S(1)} %constant_dynamic-update-slice_fusion), channel_id=1, source_target_pairs={{0,12},{2,14},{4,0},{6,2},{8,4},{10,6},{12,8},{14,10},{1,13},{3,15... | collective-permute-start | bytes 2752520 | tf_op jit(solution)/shard_map/ppermute | solution.py:26
  56.7 19.5 %all-to-all-start = ((bf16[8,64,1024]{2,1,0:T(8,128)(2,1)}), bf16[8,64,1024]{2,1,0:T(8,128)(2,1)S(1)}, u32[]{:S(2)}, u32[]{:S(2)}) async-start(bf16[8,64,1024]{2,1,0:T(8,128)(2,1)} %fusion.40), calls=%async_computation | async-start | bytes 2097152 | tf_op jit(solution)/shard_map/all_to_all | solution.py:108
  61.1 6.9 %copy-start.4 = (bf16[64,3584]{1,0:T(8,128)(2,1)S(1)}, bf16[64,3584]{1,0:T(8,128)(2,1)}, u32[]{:S(2)}) copy-start(bf16[64,3584]{1,0:T(8,128)(2,1)} %param.4) | copy-start | bytes 1376260
  61.1 6.9 %copy-start.6 = (bf16[64,3584]{1,0:T(8,128)(2,1)S(1)}, bf16[64,3584]{1,0:T(8,128)(2,1)}, u32[]{:S(2)}) copy-start(bf16[64,3584]{1,0:T(8,128)(2,1)} %copy-done.5) | copy-start | bytes 1376260
  63.3 13.2 %collective-permute-start.10 = (bf16[64,3584]{1,0:T(8,128)(2,1)}, bf16[64,3584]{1,0:T(8,128)(2,1)}, u32[]{:S(2)}, u32[]{:S(2)}) collective-permute-start(bf16[64,3584]{1,0:T(8,128)(2,1)} %get-tuple-element.63), channel_id=1, source_target_pairs={{0,4},{2,6},{4,8},{6,10},{8,12},{10,14},{12,0},{14,2},{1,5},{3,7},... | collective-permute-start | bytes 1376264 | tf_op jit(solution)/shard_map/ppermute | solution.py:26
  65.4 11.1 %collective-permute-start.11 = (bf16[64,3584]{1,0:T(8,128)(2,1)}, bf16[64,3584]{1,0:T(8,128)(2,1)}, u32[]{:S(2)}, u32[]{:S(2)}) collective-permute-start(bf16[64,3584]{1,0:T(8,128)(2,1)} %get-tuple-element.65), channel_id=1, source_target_pairs={{0,12},{2,14},{4,0},{6,2},{8,4},{10,6},{12,8},{14,10},{1,13},{3,15... | collective-permute-start | bytes 1376264 | tf_op jit(solution)/shard_map/ppermute | solution.py:26
  76.2 1.0 copy-start.2
  80.8 3.7 %copy-start = (f32[256,512]{1,0:T(8,128)S(1)}, f32[256,512]{1,0:T(8,128)}, u32[]{:S(2)}) copy-start(f32[256,512]{1,0:T(8,128)} %fusion.15) | copy-start | bytes 1572868
  80.8 3.7 %copy-start.1 = (f32[256,512]{1,0:T(8,128)S(1)}, f32[256,512]{1,0:T(8,128)}, u32[]{:S(2)}) copy-start(f32[256,512]{1,0:T(8,128)} %fusion.14) | copy-start | bytes 1572868
  86.7 16.3 %all-to-all-start.1 = ((bf16[8,64,1024]{2,1,0:T(8,128)(2,1)}), bf16[8,64,1024]{2,1,0:T(8,128)(2,1)S(1)}, u32[]{:S(2)}, u32[]{:S(2)}) async-start(bf16[8,64,1024]{2,1,0:T(8,128)(2,1)} %get-tuple-element.47), calls=%async_computation.1 | async-start | bytes 2097152 | tf_op jit(solution)/shard_map/all_to_all | solution.py:108
  91.8 12.4 %collective-permute-start.13 = (bf16[64,1024]{1,0:T(8,128)(2,1)S(1)}, bf16[64,1024]{1,0:T(8,128)(2,1)S(1)}, u32[]{:S(2)}, u32[]{:S(2)}) collective-permute-start(bf16[64,1024]{1,0:T(8,128)(2,1)S(1)} %fusion.16), channel_id=1, source_target_pairs={{0,0},{1,1},{2,16},{3,17},{4,32},{5,33},{6,48},{7,49},{8,64},{9,65... | collective-permute-start | bytes 393224 | tf_op jit(solution)/shard_map/ppermute | solution.py:43
  104.2 5.3 %collective-permute-start.15 = (bf16[64,1024]{1,0:T(8,128)(2,1)S(1)}, bf16[64,1024]{1,0:T(8,128)(2,1)S(1)}, u32[]{:S(2)}, u32[]{:S(2)}) collective-permute-start(bf16[64,1024]{1,0:T(8,128)(2,1)S(1)} %fusion.16), channel_id=1, source_target_pairs={{0,16},{16,0},{32,48},{48,32},{64,80},{80,64},{96,112},{112,96},{1... | collective-permute-start | bytes 393224 | tf_op jit(solution)/shard_map/ppermute | solution.py:26
  105.3 4.3 %collective-permute-start.14 = (bf16[64,1024]{1,0:T(8,128)(2,1)S(1)}, bf16[64,1024]{1,0:T(8,128)(2,1)S(1)}, u32[]{:S(2)}, u32[]{:S(2)}) collective-permute-start(bf16[64,1024]{1,0:T(8,128)(2,1)S(1)} %fusion.17), channel_id=1, source_target_pairs={{0,0},{1,1},{2,16},{3,17},{4,32},{5,33},{6,48},{7,49},{8,64},{9,65... | collective-permute-start | bytes 393224 | tf_op jit(solution)/shard_map/ppermute | solution.py:43
  111.2 39.9 %all-to-all-start.2 = ((bf16[8,128,1024]{2,1,0:T(8,128)(2,1)}), bf16[8,128,1024]{2,1,0:T(8,128)(2,1)S(1)}, u32[]{:S(2)}, u32[]{:S(2)}) async-start(bf16[8,128,1024]{2,1,0:T(8,128)(2,1)} %broadcast_in_dim.10), calls=%async_computation.2 | async-start | bytes 4194304 | tf_op jit(solution)/shard_map/all_to_all | solution.py:48
  127.1 6.4 %collective-permute-start.16 = (bf16[128,1024]{1,0:T(8,128)(2,1)S(1)}, bf16[128,1024]{1,0:T(8,128)(2,1)S(1)}, u32[]{:S(2)}, u32[]{:S(2)}) collective-permute-start(bf16[128,1024]{1,0:T(8,128)(2,1)S(1)} %pad_maximum_fusion.9.pair), channel_id=1, source_target_pairs={{0,32},{16,48},{32,64},{48,80},{64,96},{80,112},{96,0},{112,16},{1... | collective-permute-start | bytes 786440 | tf_op jit(solution)/shard_map/ppermute | solution.py:26
  127.1 6.5 %collective-permute-start.17 = (bf16[128,1024]{1,0:T(8,128)(2,1)S(1)}, bf16[128,1024]{1,0:T(8,128)(2,1)S(1)}, u32[]{:S(2)}, u32[]{:S(2)}) collective-permute-start(bf16[128,1024]{1,0:T(8,128)(2,1)S(1)} %pad_maximum_fusion.9.pair), channel_id=1, source_target_pairs={{0,96},{16,112},{32,0},{48,16},{64,32},{80,48},{96,64},{112,80},{1... | collective-permute-start | bytes 786440 | tf_op jit(solution)/shard_map/ppermute | solution.py:26
  133.6 5.1 %collective-permute-start.18 = (bf16[64,1024]{1,0:T(8,128)(2,1)S(1)}, bf16[64,1024]{1,0:T(8,128)(2,1)S(1)}, u32[]{:S(2)}, u32[]{:S(2)}) collective-permute-start(bf16[64,1024]{1,0:T(8,128)(2,1)S(1)} %slice.86), channel_id=1, source_target_pairs={{0,32},{16,48},{32,64},{48,80},{64,96},{80,112},{96,0},{112,16},{1... | collective-permute-start | bytes 393224 | tf_op jit(solution)/shard_map/ppermute | solution.py:26
  133.7 5.0 %collective-permute-start.19 = (bf16[64,1024]{1,0:T(8,128)(2,1)S(1)}, bf16[64,1024]{1,0:T(8,128)(2,1)S(1)}, u32[]{:S(2)}, u32[]{:S(2)}) collective-permute-start(bf16[64,1024]{1,0:T(8,128)(2,1)S(1)} %slice.87), channel_id=1, source_target_pairs={{0,96},{16,112},{32,0},{48,16},{64,32},{80,48},{96,64},{112,80},{1... | collective-permute-start | bytes 393224 | tf_op jit(solution)/shard_map/ppermute | solution.py:26
  139.4 11.7 %collective-permute-start.20 = (bf16[8,64,512]{2,1,0:T(8,128)(2,1)S(1)}, bf16[8,64,512]{2,1,0:T(8,128)(2,1)}, u32[]{:S(2)}, u32[]{:S(2)}) collective-permute-start(bf16[8,64,512]{2,1,0:T(8,128)(2,1)S(1)} %get-tuple-element.60), channel_id=1, source_target_pairs={{0,1},{1,0},{2,3},{3,2},{4,5},{5,4},{6,7},{7,6},{8,9},{9,8},{10,11... | collective-permute-start | bytes 1572872 | tf_op jit(solution)/shard_map/ppermute | solution.py:30
  151.1 9.3 %collective-permute-start.21 = (bf16[8,128,1024]{2,1,0:T(8,128)(2,1)S(1)}, bf16[8,128,1024]{2,1,0:T(8,128)(2,1)S(1)}, u32[]{:S(2)}, u32[]{:S(2)}) collective-permute-start(bf16[8,128,1024]{2,1,0:T(8,128)(2,1)S(1)} %all-to-all-done.2), channel_id=1, source_target_pairs={{0,1},{1,0},{2,3},{3,2},{4,5},{5,4},{6,7},{7,6},{8,9},{9,8},{10,11... | collective-permute-start | bytes 6291464 | tf_op jit(solution)/shard_map/ppermute | solution.py:30

commit v4 on v3

--- a/solution.py
+++ b/solution.py
@@ -170,9 +170,9 @@
     d_second = dots([d_up[n:], d_down[n:], d_across, d_side_across], dense_ws)
     part_d = joined(d_first, d_second) - part_p
     sent_d = part_d.astype(BF)
-    p, part_d, sent_d = lax.optimization_barrier((p, part_d, sent_d))
+    t_p = transposed(p)
+    p, t_p, part_d, sent_d = lax.optimization_barrier((p, t_p, part_d, sent_d))
     d = summed(sent_d, part_d)
-    t_p = transposed(p)
     d, p, t_p = lax.optimization_barrier((d, p, t_p))
     t_d = transposed(d)
     cols_pair = start_around(p, ROW)

time: 167 us -> 162 us (0.970)
  blocking collectives: 0 us -> 17.7 us
  starting transfers between devices: 68.9 us -> 59.1 us
  waiting for transfers between devices: 49.3 us -> 39.7 us
  other arithmetic: 6.19 us -> 3.58 us
    all_to_all x0 -> x1, blocking collectives: none -> 17.7 us  [summed(): came = lax.all_to_all(sent, ROW, 0, 0, tiled=True)]
    all_to_all x2 -> x1, waiting for transfers between devices: 10.5 us -> 0.01 us  [summed(): came = lax.all_to_all(sent, ROW, 0, 0, tiled=True)]
    all_to_all x2 -> x1, starting transfers between devices: 9.54 us -> 4.41 us  [summed(): came = lax.all_to_all(sent, ROW, 0, 0, tiled=True)]
    all_to_all x1, starting transfers between devices: 16 us -> 11 us  [spread(): lax.all_to_all(jnp.broadcast_to(a, (n,) + a.shape), axes, 0, 0, tiled=True)]
    convert_element_type x1, other arithmetic: 2.18 us -> 0.51 us  [local(): sent_d = part_d.astype(BF)]
  transfers between devices with their start and end apart: 25 -> 24, of which waited for: 11 -> 10; matrix products, arithmetic and copies ran while one was open for 17% -> 22% of each run, Pallas kernels for 0% -> 0%
where the time goes in v4:
time: 162 us
  starting transfers between devices  59.1 us (36%)
  waiting for transfers between devices  39.7 us (25%)
  matrix products  31.6 us (20%)
  blocking collectives  17.7 us (11%)
  local copies, waits for them, and re-layouts  8.24 us (5%)
  other arithmetic  3.58 us (2%)
    ppermute x16, waiting for transfers between devices, step(): return lax.ppermute(a, axes, pairs)  35.7 us
    ppermute x16, starting transfers between devices, step(): return lax.ppermute(a, axes, pairs)  23.4 us
    dot_general x8, matrix products, dots(): outs = [jnp.dot(a, w, preferred_element_type=F32) for w in weights]  19.8 us
    ppermute x4, starting transfers between devices, swap(): return lax.ppermute(a, 'k', [(0, 1), (1, 0)])  18.9 us
    all_to_all x1, blocking collectives, summed(): came = lax.all_to_all(sent, ROW, 0, 0, tiled=True)  17.7 us
    all_to_all x1, starting transfers between devices, spread(): lax.all_to_all(jnp.broadcast_to(a, (n,) + a.shape), axes, 0, 0, tiled=True)  11 us
    dot_general x4, matrix products, product(): return lax.dot_general(rows, cols, dims, preferred_element_type=F32)  7.74 us
    all_to_all x1, starting transfers between devices, summed(): came = lax.all_to_all(sent, ROW, 0, 0, tiled=True)  4.41 us
  transfers between devices with their start and end apart: 24, of which 10 were waited for; matrix products, arithmetic and copies ran while one was open for 22% of the time, Pallas kernels for 0%

profile of v4, /device:TPU:1, one launch (start us, length us, event | category | flops | bytes accessed | tf_op | source)
XLA Modules:
  0.0 161.6 jit_solution(4726562748870144770)
XLA Ops:
  0.6 3.8 %collective-permute-start = (bf16[64,3584]{1,0:T(8,128)(2,1)}, bf16[64,3584]{1,0:T(8,128)(2,1)S(1)}, u32[]{:S(2)}, u32[]{:S(2)}) collective-permute-start(bf16[64,3584]{1,0:T(8,128)(2,1)} %param.5), channel_id=1, source_target_pairs={{0,2},{2,0},{4,6},{6,4},{8,10},{10,8},{12,14},{14,12},{1,3},{3,1},... | collective-permute-start | bytes 1376264 | tf_op jit(solution)/shard_map/ppermute | solution.py:26
  4.5 1.6 %collective-permute-start.1 = (bf16[64,3584]{1,0:T(8,128)(2,1)}, bf16[64,3584]{1,0:T(8,128)(2,1)S(1)}, u32[]{:S(2)}, u32[]{:S(2)}) collective-permute-start(bf16[64,3584]{1,0:T(8,128)(2,1)} %param.5), channel_id=1, source_target_pairs={{0,4},{2,6},{4,8},{6,10},{8,12},{10,14},{12,0},{14,2},{1,5},{3,7},... | collective-permute-start | bytes 1376264 | tf_op jit(solution)/shard_map/ppermute | solution.py:26
  6.1 2.1 %collective-permute-start.2 = (bf16[64,3584]{1,0:T(8,128)(2,1)}, bf16[64,3584]{1,0:T(8,128)(2,1)S(1)}, u32[]{:S(2)}, u32[]{:S(2)}) collective-permute-start(bf16[64,3584]{1,0:T(8,128)(2,1)} %param.5), channel_id=1, source_target_pairs={{0,12},{2,14},{4,0},{6,2},{8,4},{10,6},{12,8},{14,10},{1,13},{3,15... | collective-permute-start | bytes 1376264 | tf_op jit(solution)/shard_map/ppermute | solution.py:26
  8.2 1.2 collective-permute-start.12
  9.5 1.8 %constant_dynamic-update-slice_fusion.5 = bf16[256,3584]{1,0:T(8,128)(2,1)} fusion(bf16[64,3584]{1,0:T(8,128)(2,1)} %param.5), kind=kLoop, calls=%fused_computation.51 | loop fusion | bytes 917504
  11.3 1.1 and_convert_fusion
  12.4 4.1 %fusion = bf16[3584,512]{1,0:T(8,128)(2,1)S(1)} fusion(bf16[3584,512]{1,0:T(8,128)(2,1)} %param.6, s32[512]{0:T(512)S(1)} %get-tuple-element.80, bf16[32,3584]{1,0:T(8,128)(2,1)S(1)} %get-tuple-element.75, bf16[32,3584]{1,0:T(8,128)(2,1)S(1)} %get-tuple-element.74, s32[512]{0:T(512)S(1)} %get-tuple-element.81), kind=kOutput, calls=%fused_computation.1 | convolution fusion | flops 245006336 | bytes 7802880 | tf_op jit(solution)/shard_map/dot_general | solution.py:59
  16.5 1.8 %collective-permute-done.1 = bf16[64,3584]{1,0:T(8,128)(2,1)S(1)} collective-permute-done((bf16[64,3584]{1,0:T(8,128)(2,1)}, bf16[64,3584]{1,0:T(8,128)(2,1)S(1)}, u32[]{:S(2)}, u32[]{:S(2)}) %collective-permute-start.1) | collective-permute-done | bytes 458784 | tf_op jit(solution)/shard_map/ppermute | solution.py:26
  18.9 2.3 %collective-permute-start.4 = (bf16[96,3584]{1,0:T(8,128)(2,1)S(1)}, bf16[96,3584]{1,0:T(8,128)(2,1)S(1)}, u32[]{:S(2)}, u32[]{:S(2)}) collective-permute-start(bf16[96,3584]{1,0:T(8,128)(2,1)S(1)} %get-tuple-element.72), channel_id=1, source_target_pairs={{0,12},{2,14},{4,0},{6,2},{8,4},{10,6},{12,8},{14,10},{1,13},{3,15... | collective-permute-start | bytes 2064392 | tf_op jit(solution)/shard_map/ppermute | solution.py:26
  21.6 2.1 %collective-permute-start.8 = (bf16[3584,512]{1,0:T(8,128)(2,1)S(1)}, bf16[3584,512]{1,0:T(8,128)(2,1)S(1)}, u32[]{:S(2)}, u32[]{:S(2)}) collective-permute-start(bf16[3584,512]{1,0:T(8,128)(2,1)S(1)} %fusion), channel_id=1, source_target_pairs={{0,1},{1,0},{2,3},{3,2},{4,5},{5,4},{6,7},{7,6},{8,9},{9,8},{10,11... | collective-permute-start | bytes 11010056 | tf_op jit(solution)/shard_map/ppermute | solution.py:30
  23.8 1.1 fusion.48
  25.0 7.7 %collective-permute-done.5 = bf16[64,3584]{1,0:T(8,128)(2,1)S(1)} collective-permute-done((bf16[64,3584]{1,0:T(8,128)(2,1)S(1)}, bf16[64,3584]{1,0:T(8,128)(2,1)S(1)}, u32[]{:S(2)}, u32[]{:S(2)}) %collective-permute-start.5) | collective-permute-done | bytes 458784 | tf_op jit(solution)/shard_map/ppermute | solution.py:26
  32.7 2.5 %collective-permute-done.3 = bf16[96,3584]{1,0:T(8,128)(2,1)S(1)} collective-permute-done((bf16[96,3584]{1,0:T(8,128)(2,1)S(1)}, bf16[96,3584]{1,0:T(8,128)(2,1)S(1)}, u32[]{:S(2)}, u32[]{:S(2)}) %collective-permute-start.3) | collective-permute-done | bytes 688160 | tf_op jit(solution)/shard_map/ppermute | solution.py:26
  36.5 2.2 %collective-permute-start.7 = (bf16[128,3584]{1,0:T(8,128)(2,1)S(1)}, bf16[128,3584]{1,0:T(8,128)(2,1)}, u32[]{:S(2)}, u32[]{:S(2)}) collective-permute-start(bf16[128,3584]{1,0:T(8,128)(2,1)S(1)} %constant_dynamic-update-slice_fusion), channel_id=1, source_target_pairs={{0,12},{2,14},{4,0},{6,2},{8,4},{10,6},{12,8},{14,10},{1,13},{3,15... | collective-permute-start | bytes 2752520 | tf_op jit(solution)/shard_map/ppermute | solution.py:26
  38.7 7.8 %collective-permute-done.9 = bf16[64,3584]{1,0:T(8,128)(2,1)S(1)} collective-permute-done((bf16[64,3584]{1,0:T(8,128)(2,1)S(1)}, bf16[64,3584]{1,0:T(8,128)(2,1)S(1)}, u32[]{:S(2)}, u32[]{:S(2)}) %collective-permute-start.9) | collective-permute-done | bytes 458784 | tf_op jit(solution)/shard_map/ppermute | solution.py:26
  46.6 1.1 fusion.50
  47.7 1.1 fusion.51
  48.8 1.1 fusion.49
  49.9 1.1 fusion.40
  51.2 5.5 %collective-permute-done.6 = bf16[128,3584]{1,0:T(8,128)(2,1)} collective-permute-done((bf16[128,3584]{1,0:T(8,128)(2,1)S(1)}, bf16[128,3584]{1,0:T(8,128)(2,1)}, u32[]{:S(2)}, u32[]{:S(2)}) %collective-permute-start.6) | collective-permute-done | bytes 917536 | tf_op jit(solution)/shard_map/ppermute | solution.py:26
  56.7 4.4 %all-to-all-start = ((bf16[8,64,1024]{2,1,0:T(8,128)(2,1)}), bf16[8,64,1024]{2,1,0:T(8,128)(2,1)S(1)}, u32[]{:S(2)}, u32[]{:S(2)}) async-start(bf16[8,64,1024]{2,1,0:T(8,128)(2,1)} %fusion.40), calls=%async_computation | async-start | bytes 2097152 | tf_op jit(solution)/shard_map/all_to_all | solution.py:108
  61.1 2.2 %fusion.42 = (bf16[64,3584]{1,0:T(8,128)(2,1)}, bf16[64,3584]{1,0:T(8,128)(2,1)}) fusion(bf16[128,3584]{1,0:T(8,128)(2,1)} %collective-permute-done.6), kind=kLoop, calls=%fused_computation.89 | loop fusion | bytes 1835008 | tf_op jit(solution)/shard_map/slice | solution.py:170
  63.4 2.0 %fusion.43 = (bf16[64,3584]{1,0:T(8,128)(2,1)S(1)}, bf16[64,3584]{1,0:T(8,128)(2,1)}) fusion(bf16[128,3584]{1,0:T(8,128)(2,1)} %collective-permute-done.7), kind=kLoop, calls=%fused_computation.90 | loop fusion | bytes 1835008 | tf_op jit(solution)/shard_map/slice | solution.py:168
  65.4 2.6 %collective-permute-start.11 = (bf16[64,3584]{1,0:T(8,128)(2,1)}, bf16[64,3584]{1,0:T(8,128)(2,1)}, u32[]{:S(2)}, u32[]{:S(2)}) collective-permute-start(bf16[64,3584]{1,0:T(8,128)(2,1)} %get-tuple-element.67), channel_id=1, source_target_pairs={{0,12},{2,14},{4,0},{6,2},{8,4},{10,6},{12,8},{14,10},{1,13},{3,15... | collective-permute-start | bytes 1376264 | tf_op jit(solution)/shard_map/ppermute | solution.py:26
  68.0 4.1 %fusion.15 = f32[256,512]{1,0:T(8,128)} fusion(bf16[3584,512]{1,0:T(8,128)(2,1)} %param.6, bf16[64,3584]{1,0:T(8,128)(2,1)S(1)} %get-tuple-element.66, bf16[64,3584]{1,0:T(8,128)(2,1)} %get-tuple-element.65, bf16[64,3584]{1,0:T(8,128)(2,1)S(1)} %copy-done.6, bf16[64,3584]{1,0:T(8,128)(2,1)S(1)} %copy-done.4), kind=kOutput, calls=%fused_computation.31 | convolution fusion | flops 946864128 | bytes 6029312 | tf_op jit(solution)/shard_map/dot_general | solution.py:66
  72.1 4.1 %fusion.14 = f32[256,512]{1,0:T(8,128)} fusion(bf16[3584,512]{1,0:T(8,128)(2,1)} %collective-permute-done.12, bf16[64,3584]{1,0:T(8,128)(2,1)S(1)} %get-tuple-element.66, bf16[64,3584]{1,0:T(8,128)(2,1)} %get-tuple-element.65, bf16[64,3584]{1,0:T(8,128)(2,1)S(1)} %copy-done.6, bf16[64,3584]{1,0:T(8,128)(2,1)S(1)} %copy-done.4), kind=kOutput, calls=%fused_computation.30 | convolution fusion | flops 946864128 | bytes 6029312 | tf_op jit(solution)/shard_map/dot_general | solution.py:66
  76.5 0.8 collective-permute-start.13
  77.4 3.6 %fusion.13 = f32[256,512]{1,0:T(8,128)S(1)} fusion(bf16[3584,512]{1,0:T(8,128)(2,1)} %param.6, bf16[64,3584]{1,0:T(8,128)(2,1)} %collective-permute-done.11, bf16[64,3584]{1,0:T(8,128)(2,1)} %collective-permute-done.10, bf16[64,3584]{1,0:T(8,128)(2,1)} %get-tuple-element.67, bf16[64,3584]{1,0:T(8,128)(2,1)S(1)} %copy-done.2), kind=kOutput, calls=%fused_computation.29 | convolution fusion | flops 946864128 | bytes 6029312 | tf_op jit(solution)/shard_map/dot_general | solution.py:66
  81.0 3.6 %fusion.12 = f32[256,512]{1,0:T(8,128)S(1)} fusion(bf16[3584,512]{1,0:T(8,128)(2,1)} %collective-permute-done.12, bf16[64,3584]{1,0:T(8,128)(2,1)} %collective-permute-done.11, bf16[64,3584]{1,0:T(8,128)(2,1)} %collective-permute-done.10, bf16[64,3584]{1,0:T(8,128)(2,1)} %get-tuple-element.67, bf16[64,3584]{1,0:T(8,128)(2,1)S(1)} %copy-done.2), kind=kOutput, calls=%fused_computation.28 | convolution fusion | flops 946864128 | bytes 6029312 | tf_op jit(solution)/shard_map/dot_general | solution.py:66
  85.2 17.7 %all_to_all.15 = bf16[8,64,1024]{2,1,0:T(8,128)(2,1)S(1)} all-to-all(bf16[8,64,1024]{2,1,0:T(8,128)(2,1)S(1)} %get-tuple-element.48), channel_id=1, replica_groups=mesh['x'=4,'yl'=2,'z'=4,'yh'=2,'k'=2] {'x','yl'}, dimensions={0} | all-to-all | bytes 2097152 | tf_op jit(solution)/shard_map/all_to_all | solution.py:108
  103.2 1.2 collective-permute-start.15
  104.4 0.7 collective-permute-start.14
  105.1 4.4 %collective-permute-done.15 = bf16[64,1024]{1,0:T(8,128)(2,1)S(1)} collective-permute-done((bf16[64,1024]{1,0:T(8,128)(2,1)S(1)}, bf16[64,1024]{1,0:T(8,128)(2,1)S(1)}, u32[]{:S(2)}, u32[]{:S(2)}) %collective-permute-start.15) | collective-permute-done | bytes 131104 | tf_op jit(solution)/shard_map/ppermute | solution.py:26
  109.5 1.6 broadcast_in_dim.10
  111.1 11.0 %all-to-all-start.2 = ((bf16[8,128,1024]{2,1,0:T(8,128)(2,1)}), bf16[8,128,1024]{2,1,0:T(8,128)(2,1)S(1)}, u32[]{:S(2)}, u32[]{:S(2)}) async-start(bf16[8,128,1024]{2,1,0:T(8,128)(2,1)} %broadcast_in_dim.10), calls=%async_computation.2 | async-start | bytes 4194304 | tf_op jit(solution)/shard_map/all_to_all | solution.py:48
  122.1 2.6 %collective-permute-start.17 = (bf16[128,1024]{1,0:T(8,128)(2,1)S(1)}, bf16[128,1024]{1,0:T(8,128)(2,1)S(1)}, u32[]{:S(2)}, u32[]{:S(2)}) collective-permute-start(bf16[128,1024]{1,0:T(8,128)(2,1)S(1)} %pad_maximum_fusion.9.pair), channel_id=1, source_target_pairs={{0,96},{16,112},{32,0},{48,16},{64,32},{80,48},{96,64},{112,80},{1... | collective-permute-start | bytes 786440 | tf_op jit(solution)/shard_map/ppermute | solution.py:26
  124.8 3.8 %collective-permute-done.16.up = bf16[128,1024]{1,0:T(8,128)(2,1)S(1)} collective-permute-done((bf16[128,1024]{1,0:T(8,128)(2,1)S(1)}, bf16[128,1024]{1,0:T(8,128)(2,1)S(1)}, u32[]{:S(2)}, u32[]{:S(2)}) %collective-permute-start.16) | collective-permute-done | bytes 262176 | tf_op jit(solution)/shard_map/ppermute | solution.py:26
  128.6 2.7 %collective-permute-start.19 = (bf16[64,1024]{1,0:T(8,128)(2,1)S(1)}, bf16[64,1024]{1,0:T(8,128)(2,1)S(1)}, u32[]{:S(2)}, u32[]{:S(2)}) collective-permute-start(bf16[64,1024]{1,0:T(8,128)(2,1)S(1)} %slice.87), channel_id=1, source_target_pairs={{0,96},{16,112},{32,0},{48,16},{64,32},{80,48},{96,64},{112,80},{1... | collective-permute-start | bytes 393224 | tf_op jit(solution)/shard_map/ppermute | solution.py:26
  131.4 2.2 %collective-permute-done.18.across = bf16[64,1024]{1,0:T(8,128)(2,1)S(1)} collective-permute-done((bf16[64,1024]{1,0:T(8,128)(2,1)S(1)}, bf16[64,1024]{1,0:T(8,128)(2,1)S(1)}, u32[]{:S(2)}, u32[]{:S(2)}) %collective-permute-start.18) | collective-permute-done | bytes 131104 | tf_op jit(solution)/shard_map/ppermute | solution.py:26
  133.6 0.6 arranged.1
  134.4 10.5 %collective-permute-start.20 = (bf16[8,64,512]{2,1,0:T(8,128)(2,1)S(1)}, bf16[8,64,512]{2,1,0:T(8,128)(2,1)}, u32[]{:S(2)}, u32[]{:S(2)}) collective-permute-start(bf16[8,64,512]{2,1,0:T(8,128)(2,1)S(1)} %get-tuple-element.62), channel_id=1, source_target_pairs={{0,1},{1,0},{2,3},{3,2},{4,5},{5,4},{6,7},{7,6},{8,9},{9,8},{10,11... | collective-permute-start | bytes 1572872 | tf_op jit(solution)/shard_map/ppermute | solution.py:30
  144.9 1.7 %collective-permute-done.20 = bf16[8,64,512]{2,1,0:T(8,128)(2,1)} collective-permute-done((bf16[8,64,512]{2,1,0:T(8,128)(2,1)S(1)}, bf16[8,64,512]{2,1,0:T(8,128)(2,1)}, u32[]{:S(2)}, u32[]{:S(2)}) %collective-permute-start.20) | collective-permute-done | bytes 524320 | tf_op jit(solution)/shard_map/ppermute | solution.py:30
  146.6 5.0 %collective-permute-start.21 = (bf16[8,128,1024]{2,1,0:T(8,128)(2,1)S(1)}, bf16[8,128,1024]{2,1,0:T(8,128)(2,1)S(1)}, u32[]{:S(2)}, u32[]{:S(2)}) collective-permute-start(bf16[8,128,1024]{2,1,0:T(8,128)(2,1)S(1)} %all-to-all-done.2), channel_id=1, source_target_pairs={{0,1},{1,0},{2,3},{3,2},{4,5},{5,4},{6,7},{7,6},{8,9},{9,8},{10,11... | collective-permute-start | bytes 6291464 | tf_op jit(solution)/shard_map/ppermute | solution.py:30
  151.6 0.7 fusion.5
  152.3 0.8 fusion.7
  153.1 2.3 %collective-permute-done.21 = bf16[8,128,1024]{2,1,0:T(8,128)(2,1)S(1)} collective-permute-done((bf16[8,128,1024]{2,1,0:T(8,128)(2,1)S(1)}, bf16[8,128,1024]{2,1,0:T(8,128)(2,1)S(1)}, u32[]{:S(2)}, u32[]{:S(2)}) %collective-permute-start.21) | collective-permute-done | bytes 2097184 | tf_op jit(solution)/shard_map/ppermute | solution.py:30
  155.3 3.1 %fusion.1 = f32[1024,512]{1,0:T(8,128)} fusion(f32[1024,512,1]{1,0,2:T(8,128)S(1)} %fusion.5, bf16[8,64,512]{2,1,0:T(8,128)(2,1)} %collective-permute-done.20, bf16[8,128,1024]{2,1,0:T(8,128)(2,1)S(1)} %collective-permute-done.21), kind=kOutput, calls=%fused_computation.5 | convolution fusion | flops 537919488 | bytes 5767168 | tf_op jit(solution)/shard_map/dot_general | solution.py:140
  158.5 3.1 %fusion.2 = f32[1024,512]{1,0:T(8,128)} fusion(f32[1024,512,1]{1,0,2:T(8,128)S(1)} %fusion.7, bf16[8,64,512]{2,1,0:T(8,128)(2,1)} %collective-permute-done.20, bf16[8,128,1024]{2,1,0:T(8,128)(2,1)S(1)} %collective-permute-done.21), kind=kOutput, calls=%fused_computation.7 | convolution fusion | flops 537919488 | bytes 5767168 | tf_op jit(solution)/shard_map/dot_general | solution.py:140
  (68 shorter events, 4.1 us)
Async XLA Ops:
  0.6 15.9 %collective-permute-start = (bf16[64,3584]{1,0:T(8,128)(2,1)}, bf16[64,3584]{1,0:T(8,128)(2,1)S(1)}, u32[]{:S(2)}, u32[]{:S(2)}) collective-permute-start(bf16[64,3584]{1,0:T(8,128)(2,1)} %param.5), channel_id=1, source_target_pairs={{0,2},{2,0},{4,6},{6,4},{8,10},{10,8},{12,14},{14,12},{1,3},{3,1},... | collective-permute-start | bytes 1376264 | tf_op jit(solution)/shard_map/ppermute | solution.py:26
  4.5 13.9 %collective-permute-start.1 = (bf16[64,3584]{1,0:T(8,128)(2,1)}, bf16[64,3584]{1,0:T(8,128)(2,1)S(1)}, u32[]{:S(2)}, u32[]{:S(2)}) collective-permute-start(bf16[64,3584]{1,0:T(8,128)(2,1)} %param.5), channel_id=1, source_target_pairs={{0,4},{2,6},{4,8},{6,10},{8,12},{10,14},{12,0},{14,2},{1,5},{3,7},... | collective-permute-start | bytes 1376264 | tf_op jit(solution)/shard_map/ppermute | solution.py:26
  6.1 12.3 %collective-permute-start.2 = (bf16[64,3584]{1,0:T(8,128)(2,1)}, bf16[64,3584]{1,0:T(8,128)(2,1)S(1)}, u32[]{:S(2)}, u32[]{:S(2)}) collective-permute-start(bf16[64,3584]{1,0:T(8,128)(2,1)} %param.5), channel_id=1, source_target_pairs={{0,12},{2,14},{4,0},{6,2},{8,4},{10,6},{12,8},{14,10},{1,13},{3,15... | collective-permute-start | bytes 1376264 | tf_op jit(solution)/shard_map/ppermute | solution.py:26
  8.2 63.9 %collective-permute-start.12 = (bf16[3584,512]{1,0:T(8,128)(2,1)}, bf16[3584,512]{1,0:T(8,128)(2,1)}, u32[]{:S(2)}, u32[]{:S(2)}) collective-permute-start(bf16[3584,512]{1,0:T(8,128)(2,1)} %param.6), channel_id=1, source_target_pairs={{0,1},{1,0},{2,3},{3,2},{4,5},{5,4},{6,7},{7,6},{8,9},{9,8},{10,11... | collective-permute-start | bytes 11010056 | tf_op jit(solution)/shard_map/ppermute | solution.py:30
  12.4 4.1 %copy-start.3 = (bf16[64,3584]{1,0:T(8,128)(2,1)S(1)}, bf16[64,3584]{1,0:T(8,128)(2,1)}, u32[]{:S(2)}) copy-start(bf16[64,3584]{1,0:T(8,128)(2,1)} %param.4) | copy-start | bytes 1376260
  16.5 7.3 %copy-start.7 = (bf16[256,3584]{1,0:T(8,128)(2,1)S(1)}, bf16[256,3584]{1,0:T(8,128)(2,1)}, u32[]{:S(2)}) copy-start(bf16[256,3584]{1,0:T(8,128)(2,1)} %constant_dynamic-update-slice_fusion.5) | copy-start | bytes 5505028
  18.5 16.7 %collective-permute-start.3 = (bf16[96,3584]{1,0:T(8,128)(2,1)S(1)}, bf16[96,3584]{1,0:T(8,128)(2,1)S(1)}, u32[]{:S(2)}, u32[]{:S(2)}) collective-permute-start(bf16[96,3584]{1,0:T(8,128)(2,1)S(1)} %get-tuple-element.73), channel_id=1, source_target_pairs={{0,4},{2,6},{4,8},{6,10},{8,12},{10,14},{12,0},{14,2},{1,5},{3,7},... | collective-permute-start | bytes 2064392 | tf_op jit(solution)/shard_map/ppermute | solution.py:26
  18.9 16.3 %collective-permute-start.4 = (bf16[96,3584]{1,0:T(8,128)(2,1)S(1)}, bf16[96,3584]{1,0:T(8,128)(2,1)S(1)}, u32[]{:S(2)}, u32[]{:S(2)}) collective-permute-start(bf16[96,3584]{1,0:T(8,128)(2,1)S(1)} %get-tuple-element.72), channel_id=1, source_target_pairs={{0,12},{2,14},{4,0},{6,2},{8,4},{10,6},{12,8},{14,10},{1,13},{3,15... | collective-permute-start | bytes 2064392 | tf_op jit(solution)/shard_map/ppermute | solution.py:26
  21.3 11.4 %collective-permute-start.5 = (bf16[64,3584]{1,0:T(8,128)(2,1)S(1)}, bf16[64,3584]{1,0:T(8,128)(2,1)S(1)}, u32[]{:S(2)}, u32[]{:S(2)}) collective-permute-start(bf16[64,3584]{1,0:T(8,128)(2,1)S(1)} %copy-done.3), channel_id=1, source_target_pairs={{0,2},{2,0},{4,6},{6,4},{8,10},{10,8},{12,14},{14,12},{1,3},{3,1},... | collective-permute-start | bytes 1376264 | tf_op jit(solution)/shard_map/ppermute | solution.py:26
  21.6 26.0 %collective-permute-start.8 = (bf16[3584,512]{1,0:T(8,128)(2,1)S(1)}, bf16[3584,512]{1,0:T(8,128)(2,1)S(1)}, u32[]{:S(2)}, u32[]{:S(2)}) collective-permute-start(bf16[3584,512]{1,0:T(8,128)(2,1)S(1)} %fusion), channel_id=1, source_target_pairs={{0,1},{1,0},{2,3},{3,2},{4,5},{5,4},{6,7},{7,6},{8,9},{9,8},{10,11... | collective-permute-start | bytes 11010056 | tf_op jit(solution)/shard_map/ppermute | solution.py:30
  32.7 3.3 %copy-start.5 = (bf16[64,3584]{1,0:T(8,128)(2,1)}, bf16[64,3584]{1,0:T(8,128)(2,1)S(1)}, u32[]{:S(2)}) copy-start(bf16[64,3584]{1,0:T(8,128)(2,1)S(1)} %collective-permute-done.5) | copy-start | bytes 1376260
  35.4 11.1 %collective-permute-start.9 = (bf16[64,3584]{1,0:T(8,128)(2,1)S(1)}, bf16[64,3584]{1,0:T(8,128)(2,1)S(1)}, u32[]{:S(2)}, u32[]{:S(2)}) collective-permute-start(bf16[64,3584]{1,0:T(8,128)(2,1)S(1)} %pad_maximum_fusion.4), channel_id=1, source_target_pairs={{0,2},{2,0},{4,6},{6,4},{8,10},{10,8},{12,14},{14,12},{1,3},{3,1},... | collective-permute-start | bytes 1376264 | tf_op jit(solution)/shard_map/ppermute | solution.py:26
  36.0 20.7 %collective-permute-start.6 = (bf16[128,3584]{1,0:T(8,128)(2,1)S(1)}, bf16[128,3584]{1,0:T(8,128)(2,1)}, u32[]{:S(2)}, u32[]{:S(2)}) collective-permute-start(bf16[128,3584]{1,0:T(8,128)(2,1)S(1)} %constant_dynamic-update-slice_fusion), channel_id=1, source_target_pairs={{0,4},{2,6},{4,8},{6,10},{8,12},{10,14},{12,0},{14,2},{1,5},{3,7},... | collective-permute-start | bytes 2752520 | tf_op jit(solution)/shard_map/ppermute | solution.py:26
  36.5 20.1 %collective-permute-start.7 = (bf16[128,3584]{1,0:T(8,128)(2,1)S(1)}, bf16[128,3584]{1,0:T(8,128)(2,1)}, u32[]{:S(2)}, u32[]{:S(2)}) collective-permute-start(bf16[128,3584]{1,0:T(8,128)(2,1)S(1)} %constant_dynamic-update-slice_fusion), channel_id=1, source_target_pairs={{0,12},{2,14},{4,0},{6,2},{8,4},{10,6},{12,8},{14,10},{1,13},{3,15... | collective-permute-start | bytes 2752520 | tf_op jit(solution)/shard_map/ppermute | solution.py:26
  56.7 19.5 %all-to-all-start = ((bf16[8,64,1024]{2,1,0:T(8,128)(2,1)}), bf16[8,64,1024]{2,1,0:T(8,128)(2,1)S(1)}, u32[]{:S(2)}, u32[]{:S(2)}) async-start(bf16[8,64,1024]{2,1,0:T(8,128)(2,1)} %fusion.40), calls=%async_computation | async-start | bytes 2097152 | tf_op jit(solution)/shard_map/all_to_all | solution.py:108
  61.1 6.9 %copy-start.4 = (bf16[64,3584]{1,0:T(8,128)(2,1)S(1)}, bf16[64,3584]{1,0:T(8,128)(2,1)}, u32[]{:S(2)}) copy-start(bf16[64,3584]{1,0:T(8,128)(2,1)} %param.4) | copy-start | bytes 1376260
  61.1 6.9 %copy-start.6 = (bf16[64,3584]{1,0:T(8,128)(2,1)S(1)}, bf16[64,3584]{1,0:T(8,128)(2,1)}, u32[]{:S(2)}) copy-start(bf16[64,3584]{1,0:T(8,128)(2,1)} %copy-done.5) | copy-start | bytes 1376260
  63.3 13.2 %collective-permute-start.10 = (bf16[64,3584]{1,0:T(8,128)(2,1)}, bf16[64,3584]{1,0:T(8,128)(2,1)}, u32[]{:S(2)}, u32[]{:S(2)}) collective-permute-start(bf16[64,3584]{1,0:T(8,128)(2,1)} %get-tuple-element.65), channel_id=1, source_target_pairs={{0,4},{2,6},{4,8},{6,10},{8,12},{10,14},{12,0},{14,2},{1,5},{3,7},... | collective-permute-start | bytes 1376264 | tf_op jit(solution)/shard_map/ppermute | solution.py:26
  65.4 11.1 %collective-permute-start.11 = (bf16[64,3584]{1,0:T(8,128)(2,1)}, bf16[64,3584]{1,0:T(8,128)(2,1)}, u32[]{:S(2)}, u32[]{:S(2)}) collective-permute-start(bf16[64,3584]{1,0:T(8,128)(2,1)} %get-tuple-element.67), channel_id=1, source_target_pairs={{0,12},{2,14},{4,0},{6,2},{8,4},{10,6},{12,8},{14,10},{1,13},{3,15... | collective-permute-start | bytes 1376264 | tf_op jit(solution)/shard_map/ppermute | solution.py:26
  76.2 1.2 copy-start.2
  76.5 8.7 %collective-permute-start.13 = (bf16[64,1024]{1,0:T(8,128)(2,1)S(1)}, bf16[64,1024]{1,0:T(8,128)(2,1)S(1)}, u32[]{:S(2)}, u32[]{:S(2)}) collective-permute-start(bf16[64,1024]{1,0:T(8,128)(2,1)S(1)} %fusion.16), channel_id=1, source_target_pairs={{0,0},{1,1},{2,16},{3,17},{4,32},{5,33},{6,48},{7,49},{8,64},{9,65... | collective-permute-start | bytes 393224 | tf_op jit(solution)/shard_map/ppermute | solution.py:43
  81.0 3.7 %copy-start = (f32[256,512]{1,0:T(8,128)S(1)}, f32[256,512]{1,0:T(8,128)}, u32[]{:S(2)}) copy-start(f32[256,512]{1,0:T(8,128)} %fusion.15) | copy-start | bytes 1572868
  81.0 3.7 %copy-start.1 = (f32[256,512]{1,0:T(8,128)S(1)}, f32[256,512]{1,0:T(8,128)}, u32[]{:S(2)}) copy-start(f32[256,512]{1,0:T(8,128)} %fusion.14) | copy-start | bytes 1572868
  103.2 6.3 %collective-permute-start.15 = (bf16[64,1024]{1,0:T(8,128)(2,1)S(1)}, bf16[64,1024]{1,0:T(8,128)(2,1)S(1)}, u32[]{:S(2)}, u32[]{:S(2)}) collective-permute-start(bf16[64,1024]{1,0:T(8,128)(2,1)S(1)} %fusion.16), channel_id=1, source_target_pairs={{0,16},{16,0},{32,48},{48,32},{64,80},{80,64},{96,112},{112,96},{1... | collective-permute-start | bytes 393224 | tf_op jit(solution)/shard_map/ppermute | solution.py:26
  104.4 5.1 %collective-permute-start.14 = (bf16[64,1024]{1,0:T(8,128)(2,1)S(1)}, bf16[64,1024]{1,0:T(8,128)(2,1)S(1)}, u32[]{:S(2)}, u32[]{:S(2)}) collective-permute-start(bf16[64,1024]{1,0:T(8,128)(2,1)S(1)} %fusion.17), channel_id=1, source_target_pairs={{0,0},{1,1},{2,16},{3,17},{4,32},{5,33},{6,48},{7,49},{8,64},{9,65... | collective-permute-start | bytes 393224 | tf_op jit(solution)/shard_map/ppermute | solution.py:43
  111.1 35.4 %all-to-all-start.2 = ((bf16[8,128,1024]{2,1,0:T(8,128)(2,1)}), bf16[8,128,1024]{2,1,0:T(8,128)(2,1)S(1)}, u32[]{:S(2)}, u32[]{:S(2)}) async-start(bf16[8,128,1024]{2,1,0:T(8,128)(2,1)} %broadcast_in_dim.10), calls=%async_computation.2 | async-start | bytes 4194304 | tf_op jit(solution)/shard_map/all_to_all | solution.py:48
  122.1 6.4 %collective-permute-start.16 = (bf16[128,1024]{1,0:T(8,128)(2,1)S(1)}, bf16[128,1024]{1,0:T(8,128)(2,1)S(1)}, u32[]{:S(2)}, u32[]{:S(2)}) collective-permute-start(bf16[128,1024]{1,0:T(8,128)(2,1)S(1)} %pad_maximum_fusion.9.pair), channel_id=1, source_target_pairs={{0,32},{16,48},{32,64},{48,80},{64,96},{80,112},{96,0},{112,16},{1... | collective-permute-start | bytes 786440 | tf_op jit(solution)/shard_map/ppermute | solution.py:26
  122.1 6.5 %collective-permute-start.17 = (bf16[128,1024]{1,0:T(8,128)(2,1)S(1)}, bf16[128,1024]{1,0:T(8,128)(2,1)S(1)}, u32[]{:S(2)}, u32[]{:S(2)}) collective-permute-start(bf16[128,1024]{1,0:T(8,128)(2,1)S(1)} %pad_maximum_fusion.9.pair), channel_id=1, source_target_pairs={{0,96},{16,112},{32,0},{48,16},{64,32},{80,48},{96,64},{112,80},{1... | collective-permute-start | bytes 786440 | tf_op jit(solution)/shard_map/ppermute | solution.py:26
  128.5 5.1 %collective-permute-start.18 = (bf16[64,1024]{1,0:T(8,128)(2,1)S(1)}, bf16[64,1024]{1,0:T(8,128)(2,1)S(1)}, u32[]{:S(2)}, u32[]{:S(2)}) collective-permute-start(bf16[64,1024]{1,0:T(8,128)(2,1)S(1)} %slice.86), channel_id=1, source_target_pairs={{0,32},{16,48},{32,64},{48,80},{64,96},{80,112},{96,0},{112,16},{1... | collective-permute-start | bytes 393224 | tf_op jit(solution)/shard_map/ppermute | solution.py:26
  128.6 5.0 %collective-permute-start.19 = (bf16[64,1024]{1,0:T(8,128)(2,1)S(1)}, bf16[64,1024]{1,0:T(8,128)(2,1)S(1)}, u32[]{:S(2)}, u32[]{:S(2)}) collective-permute-start(bf16[64,1024]{1,0:T(8,128)(2,1)S(1)} %slice.87), channel_id=1, source_target_pairs={{0,96},{16,112},{32,0},{48,16},{64,32},{80,48},{96,64},{112,80},{1... | collective-permute-start | bytes 393224 | tf_op jit(solution)/shard_map/ppermute | solution.py:26
  134.4 12.2 %collective-permute-start.20 = (bf16[8,64,512]{2,1,0:T(8,128)(2,1)S(1)}, bf16[8,64,512]{2,1,0:T(8,128)(2,1)}, u32[]{:S(2)}, u32[]{:S(2)}) collective-permute-start(bf16[8,64,512]{2,1,0:T(8,128)(2,1)S(1)} %get-tuple-element.62), channel_id=1, source_target_pairs={{0,1},{1,0},{2,3},{3,2},{4,5},{5,4},{6,7},{7,6},{8,9},{9,8},{10,11... | collective-permute-start | bytes 1572872 | tf_op jit(solution)/shard_map/ppermute | solution.py:30
  146.6 8.8 %collective-permute-start.21 = (bf16[8,128,1024]{2,1,0:T(8,128)(2,1)S(1)}, bf16[8,128,1024]{2,1,0:T(8,128)(2,1)S(1)}, u32[]{:S(2)}, u32[]{:S(2)}) collective-permute-start(bf16[8,128,1024]{2,1,0:T(8,128)(2,1)S(1)} %all-to-all-done.2), channel_id=1, source_target_pairs={{0,1},{1,0},{2,3},{3,2},{4,5},{5,4},{6,7},{7,6},{8,9},{9,8},{10,11... | collective-permute-start | bytes 6291464 | tf_op jit(solution)/shard_map/ppermute | solution.py:30
